TPU v7x, 32 devices: a whole 2x2x4 slice. The times are simulated.
32 devices in a mesh: dp: 16 (over z, x, core), tensor: 2 (over y).
Axes of the slice: x: 2, y: 2, z: 4, core: 2. Of those that a mesh axis runs over, the one named last changes fastest.
Arguments:
- tokens: bfloat16 [6144, 1024], P(('dp', 'tensor')), may hold values from -6 to 6
- cotangent: bfloat16 [6144, 1024], P(('dp', 'tensor')), may hold values from -6 to 6
- seq_lengths: int32 [16, 8], P('dp'), may hold values from 0 to 384, as said below
- norm1_gain: float32 [1024], replicated, may hold values from 0.5 to 1.5
- norm2_gain: float32 [1024], replicated, may hold values from 0.5 to 1.5
- mixer_in: bfloat16 [1024, 2, 1536], P(None, None, 'tensor'), may hold values from -0.1875 to 0.1875
- state_in: bfloat16 [1024, 256], replicated, may hold values from -0.1875 to 0.1875
- step_in: bfloat16 [1024, 24], P(None, 'tensor'), may hold values from -0.375 to 0.375
- conv_inner: float32 [4, 1536], P(None, 'tensor'), may hold values from -3 to 3
- conv_state: float32 [4, 256], replicated, may hold values from -3 to 3
- step_bias: float32 [24], P('tensor'), may hold values from -4 to -2
- decay_log: float32 [24], P('tensor'), may hold values from -3 to 0.5
- skip_gain: float32 [24], P('tensor'), may hold values from 0.5 to 1.5
- mixer_out: bfloat16 [1024, 1536], P(None, 'tensor'), may hold values from -0.4375 to 0.4375
- query_in: bfloat16 [1024, 512], P(None, 'tensor'), may hold values from -0.1875 to 0.1875
- key_value: bfloat16 [1024, 2, 128], replicated, may hold values from -0.1875 to 0.1875
- attend_out: bfloat16 [1024, 512], P(None, 'tensor'), may hold values from -2 to 2
- gate_up: bfloat16 [1024, 2, 2048], P(None, None, 'tensor'), may hold values from -0.1875 to 0.1875
- down_out: bfloat16 [1024, 2048], P(None, 'tensor'), may hold values from -0.125 to 0.125
Outputs:
- block_out: bfloat16 [6144, 1024], P(('dp', 'tensor'))
- token_grad: bfloat16 [6144, 1024], P(('dp', 'tensor'))
- grad_norm1: float32 [1024], replicated
- grad_norm2: float32 [1024], replicated
- grad_mixer_in: float32 [1024, 2, 1536], P('dp', None, 'tensor')
- grad_state_in: float32 [1024, 256], P('dp')
- grad_step_in: float32 [1024, 24], P('dp', 'tensor')
- grad_conv_inner: float32 [4, 1536], P(None, 'tensor')
- grad_conv_state: float32 [4, 256], replicated
- grad_step_bias: float32 [24], P('tensor')
- grad_decay_log: float32 [24], P('tensor')
- grad_skip_gain: float32 [24], P('tensor')
- grad_mixer_out: float32 [1024, 1536], P('dp', 'tensor')
- grad_query_in: float32 [1024, 512], P('dp', 'tensor')
- grad_key_value: float32 [1024, 2, 128], P('dp')
- grad_attend_out: float32 [1024, 512], P('dp', 'tensor')
- grad_gate_up: float32 [1024, 2, 2048], P('dp', None, 'tensor')
- grad_down_out: float32 [1024, 2048], P('dp', 'tensor')
Inputs may be any that keep to these rules, and one draw needn't show every extreme that they name: `seq_lengths`: row g lists the lengths of the sequences of data group g in the order they lie in its 384 slots, then zeros; a row has 1 to 8 sequences and its lengths sum to at least 192; in some row one sequence fills all 384 slots.
All inputs are finite; a program needn't handle non-finite values.
Results may differ from a plain program's by a relative error of at most 0.018.
Values may be sent and summed in bfloat16 or wider, within the bound.
No kernel may reach another device: no remote copies, remote signals or barrier semaphores. Data moves between devices by JAX's collectives and lax.ppermute only.
A program may use at most 128 MiB of HBM per device.

v0:
```python
import functools

import jax
import jax.numpy as jnp
from jax import lax
from jax.experimental import pallas as pl
from jax.experimental.pallas import tpu as pltpu
from jax.sharding import PartitionSpec as P

HD = 64
QH = 8
KVH = 2
LANES = 128

rope_base = 100000000000.0
norm_eps = 1e-05
far = -1e30
highest = lax.Precision.HIGHEST
f32 = jnp.float32
bf16 = jnp.bfloat16


def padded(width):
    return -(-width // LANES) * LANES


def pad_to(values, width):
    return jnp.pad(values, [(0, 0)] * (values.ndim - 1) + [(0, width - values.shape[-1])])


def mm(left, right):
    return jnp.dot(left, right, preferred_element_type=f32)


def mm_nt(left, right):
    return lax.dot_general(left, right, (((1,), (1,)), ((), ())), preferred_element_type=f32)


def mm_tn(left, right):
    return lax.dot_general(left, right, (((0,), (0,)), ((), ())), preferred_element_type=f32)


def mm_exact(left, right):
    return jnp.dot(left, right, preferred_element_type=f32, precision=highest)


def lane_ids(rows):
    return lax.broadcasted_iota(jnp.int32, (rows, LANES), 1)


def partner_half(values):
    lane = lane_ids(values.shape[0])
    return jnp.where(lane % HD < HD // 2, pltpu.roll(values, LANES - HD // 2, 1), pltpu.roll(values, HD // 2, 1))


def rotated(values, cosine, signed_sine):
    return values * cosine + partner_half(values) * signed_sine


def conv_terms(values, masks):
    return [pltpu.roll(values, offset, 0) * masks[offset] for offset in (3, 2, 1)] + [values]


def conv_back(grad, masks, taps):
    rows = grad.shape[0]
    total = grad * taps[3:4]
    for offset in (1, 2, 3):
        total = total + pltpu.roll(grad * masks[offset], rows - offset, 0) * taps[3 - offset : 4 - offset]
    return total


def link_bias(seq_col, seq_row, transposed):
    rows = seq_col.shape[0]
    down = lax.broadcasted_iota(jnp.int32, (rows, rows), 0)
    across = lax.broadcasted_iota(jnp.int32, (rows, rows), 1)
    ordered = down <= across if transposed else down >= across
    return (seq_col == seq_row) & ordered


def step_parts(raw, bias):
    shifted = raw + bias
    return jnp.maximum(shifted, 0.0) + jnp.log1p(jnp.exp(-jnp.abs(shifted)))


def spread_heads(columns, first, width):
    rows = columns.shape[0]
    low = jnp.broadcast_to(columns[:, first : first + 1], (rows, LANES))
    if width <= HD:
        return low
    high = jnp.broadcast_to(columns[:, first + 1 : first + 2], (rows, LANES))
    return jnp.where(lane_ids(rows) < HD, low, high)


def half_mask(rows, side):
    lane = lane_ids(rows)
    return lane < HD if side == 0 else lane >= HD


def front_kernel(
    dims, place_ref, own_ref, other_ref, wbc_ref, wsp_ref, wzx_ref, wq_ref, wmix_ref, watt_ref, gain_ref, seqc_ref,
    seqr_ref, masks_ref, cos_ref, sin_ref, convx_ref, convs_ref, bias_ref, rate_ref, skip_ref,
    x_ref, act_ref, pa_ref, pb_ref, y_ref, cat_ref, part_ref, neg_ref, g_ref, xdt_ref,
):
    heads, qheads, wp, qwp, span = dims
    rows = x_ref.shape[0]
    share = own_ref.shape[0]
    if share == rows:
        x_ref[...] = own_ref[...]
    else:
        x_ref[pl.ds(pl.multiple_of(place_ref[0] * share, 16), share), :] = own_ref[...]
        x_ref[pl.ds(pl.multiple_of(place_ref[1] * share, 16), share), :] = other_ref[...]
    finish(x_ref)
    x = x_ref[...].astype(f32)
    act = (x * lax.rsqrt(jnp.mean(x * x, axis=-1, keepdims=True) + norm_eps) * gain_ref[...]).astype(bf16)
    act_ref[...] = act
    finish(act_ref)
    pb_ref[:, wp : wp + 256] = mm(act, wbc_ref[...])
    pb_ref[:, wp + 256 :] = mm(act, wsp_ref[:, :LANES])
    pb_ref[:, :wp] = mm(act, wzx_ref[:, wp:])
    pa_ref[:, wp : wp + qwp] = mm(act, wq_ref[...])
    pa_ref[:, wp + qwp :] = mm(act, wsp_ref[:, LANES:])
    pa_ref[:, :wp] = mm(act, wzx_ref[:, :wp])
    finish(pa_ref, pb_ref)
    masks = {k: masks_ref[:, k : k + 1] for k in (1, 2, 3)}
    linked = link_bias(seqc_ref[...], seqr_ref[...], False)
    neg_ref[...] = jnp.where(linked, 0.0, far)
    dt = step_parts(pb_ref[:, wp + 256 :], bias_ref[...])
    decay = mm_exact(jnp.where(linked, 1.0, 0.0), -dt * rate_ref[...])
    decay_t = decay.T
    terms = conv_terms(pb_ref[:, wp : wp + 256], masks)
    bcc = sum(t * convs_ref[k : k + 1, :] for k, t in enumerate(terms))
    bcc = (bcc * jax.nn.sigmoid(bcc)).astype(bf16)
    g_ref[...] = mm_nt(bcc[:, 128:], bcc[:, :128])

    for p in range(wp // LANES):
        cols = slice(p * LANES, (p + 1) * LANES)
        width = HD * min(2, heads - 2 * p)
        conv = sum(t * convx_ref[k : k + 1, cols] for k, t in enumerate(conv_terms(pb_ref[:, cols], masks)))
        xc = conv * jax.nn.sigmoid(conv)
        xdt_ref[...] = (xc * spread_heads(dt, 2 * p, width)).astype(bf16)
        blocks = []
        for a in range(rows // span):
            here = slice(a * span, (a + 1) * span)
            reach = (a + 1) * span
            sides = []
            for h in range(2 * p, 2 * p + width // HD):
                gap = decay[here, h : h + 1] - decay_t[h : h + 1, :reach]
                mixing = g_ref[here, :reach] * jnp.exp(gap + neg_ref[here, :reach])
                sides.append(mm(mixing.astype(bf16), xdt_ref[:reach, :]))
            blocks.append(sides[0] if len(sides) == 1 else jnp.where(half_mask(span, 0), sides[0], sides[1]))
        y = jnp.concatenate(blocks, axis=0) + skip_ref[:, cols] * xc
        y_ref[:, cols] = y
        z = pa_ref[:, cols]
        cat_ref[:, cols] = (y * (z * jax.nn.sigmoid(z))).astype(bf16)

    finish(y_ref)
    cosine, sine = cos_ref[...], sin_ref[...]
    pair = pa_ref[:, wp + qwp :]
    swapped = pltpu.roll(pair, HD, 1)
    lower = half_mask(rows, 0)
    keys = rotated(jnp.where(lower, pair, swapped), cosine, sine).astype(bf16)
    values = jnp.where(lower, swapped, pair).astype(bf16)
    for p in range(qwp // LANES):
        cols = slice(wp + p * LANES, wp + (p + 1) * LANES)
        queries = rotated(pa_ref[:, cols], cosine, sine).astype(bf16)
        for a in range(rows // span):
            here = slice(a * span, (a + 1) * span)
            reach = (a + 1) * span
            sides = []
            for side in range(min(2, qheads - 2 * p)):
                q = jnp.where(half_mask(span, side), queries[here], jnp.zeros((), bf16))
                scores = mm_nt(q, keys[:reach]) * (HD**-0.5) + neg_ref[here, :reach]
                weights = jnp.exp(scores - jnp.max(scores, axis=-1, keepdims=True))
                probs = weights / jnp.sum(weights, axis=-1, keepdims=True)
                sides.append(mm(probs.astype(bf16), values[:reach]))
            if len(sides) == 1:
                out = jnp.where(half_mask(span, 0), sides[0], 0.0)
            else:
                out = jnp.where(half_mask(span, 0), sides[0], sides[1])
            cat_ref[here, cols] = out.astype(bf16)
    finish(cat_ref)
    part_ref[...] = (mm_nt(cat_ref[:, :wp], wmix_ref[...]) + mm_nt(cat_ref[:, wp:], watt_ref[...])).astype(bf16)


def middle_kernel(
    x_ref, own_ref, other_ref, gain_ref, wgu_ref, down_ref, dhid_ref,
    h1_ref, n2_ref, hidden_ref, dgu_ref, out_ref, dn2_ref,
):
    width = down_ref.shape[1]
    h1 = x_ref[...].astype(f32) + (own_ref[...].astype(f32) + other_ref[...].astype(f32))
    h1_ref[...] = h1
    finish(h1_ref)
    n2 = (h1 * lax.rsqrt(jnp.mean(h1 * h1, axis=-1, keepdims=True) + norm_eps) * gain_ref[...]).astype(bf16)
    n2_ref[...] = n2
    finish(n2_ref)
    gate = mm(n2, wgu_ref[:, :width])
    up = mm(n2, wgu_ref[:, width:])
    sig = jax.nn.sigmoid(gate)
    silu = gate * sig
    hidden = (silu * up).astype(bf16)
    hidden_ref[...] = hidden
    finish(hidden_ref)
    dhid = dhid_ref[...].astype(f32)
    dgu_ref[:, :width] = (dhid * up * (sig * (1.0 + gate * (1.0 - sig)))).astype(bf16)
    dgu_ref[:, width:] = (dhid * silu).astype(bf16)
    finish(dgu_ref)
    dn2_ref[...] = mm_nt(dgu_ref[...], wgu_ref[...]).astype(bf16)
    finish(dn2_ref)
    out_ref[...] = mm_nt(hidden, down_ref[...]).astype(bf16)


def attend_back_kernel(
    dims, share, place_ref, own_ref, other_ref, ffn_ref, h1_ref, dout_ref, gain2_ref, wmix_ref, watt_ref, seqc_ref,
    seqr_ref, cos_ref, sin_ref, pa_ref, y_ref,
    dh1_ref, ffn_send_ref, dmix_ref, dy_ref, da_ref, gn2_ref,
    neg_ref, dh1_all_ref, datt_ref, dk_ref, dv_ref,
):
    heads, qheads, wp, qwp, span = dims
    rows = own_ref.shape[0]
    dn2 = own_ref[...].astype(f32) + other_ref[...].astype(f32)
    h1 = h1_ref[...]
    r2 = lax.rsqrt(jnp.mean(h1 * h1, axis=-1, keepdims=True) + norm_eps)
    u = dn2 * gain2_ref[...]
    dh1 = dout_ref[...].astype(f32) + r2 * u - h1 * (r2 * r2 * r2 * jnp.mean(u * h1, axis=-1, keepdims=True))
    gn2_ref[...] = jnp.sum(dn2 * h1 * r2, axis=0, keepdims=True)
    dh1_all_ref[...] = dh1
    dh1_ref[...] = dh1_all_ref[pl.ds(pl.multiple_of(place_ref[0] * share, 16), share), :]
    ffn_send_ref[...] = ffn_ref[pl.ds(pl.multiple_of(place_ref[1] * share, 16), share), :]
    dmix = dh1.astype(bf16)
    dmix_ref[...] = dmix
    finish(dh1_ref, ffn_send_ref, dmix_ref)
    datt_ref[...] = mm(dmix, watt_ref[...]).astype(bf16)
    for p in range(wp // LANES):
        cols = slice(p * LANES, (p + 1) * LANES)
        dgated = mm(dmix, wmix_ref[:, cols])
        z = pa_ref[:, cols]
        sig = jax.nn.sigmoid(z)
        dy_ref[:, cols] = dgated * (z * sig)
        da_ref[:, cols] = (dgated * y_ref[:, cols] * (sig * (1.0 + z * (1.0 - sig)))).astype(bf16)
    finish(dy_ref)

    linked_t = link_bias(seqc_ref[...], seqr_ref[...], True)
    neg_ref[...] = jnp.where(linked_t, 0.0, far)
    lower = half_mask(rows, 0)
    cosine, sine = cos_ref[...], sin_ref[...]
    pair = pa_ref[:, wp + qwp :]
    swapped = pltpu.roll(pair, HD, 1)
    keys = rotated(jnp.where(lower, pair, swapped), cosine, sine).astype(bf16)
    values = jnp.where(lower, swapped, pair).astype(bf16)
    dk_ref[...] = jnp.zeros_like(dk_ref)
    dv_ref[...] = jnp.zeros_like(dv_ref)
    for p in range(qwp // LANES):
        cols = slice(wp + p * LANES, wp + (p + 1) * LANES)
        queries = rotated(pa_ref[:, cols], cosine, sine).astype(bf16)
        datt = datt_ref[:, p * LANES : (p + 1) * LANES]
        blocks = []
        for a in range(rows // span):
            here = slice(a * span, (a + 1) * span)
            reach = (a + 1) * span
            sides = []
            for side in range(min(2, qheads - 2 * p)):
                half = half_mask(span, side)
                q = jnp.where(half, queries[here], jnp.zeros((), bf16))
                do = jnp.where(half, datt[here], jnp.zeros((), bf16))
                scores = mm_nt(keys[:reach], q) * (HD**-0.5) + neg_ref[:reach, here]
                weights = jnp.exp(scores - jnp.max(scores, axis=0, keepdims=True))
                probs = weights / jnp.sum(weights, axis=0, keepdims=True)
                dp = mm_nt(values[:reach], do)
                ds = (probs * (dp - jnp.sum(probs * dp, axis=0, keepdims=True))).astype(bf16)
                dk_ref[:reach, :] += mm(ds, q)
                dv_ref[:reach, :] += mm(probs.astype(bf16), do)
                sides.append(mm_tn(ds, keys[:reach]))
            if len(sides) == 1:
                blocks.append(jnp.where(half_mask(span, 0), sides[0], 0.0))
            else:
                blocks.append(jnp.where(half_mask(span, 0), sides[0], sides[1]))
        dq = jnp.concatenate(blocks, axis=0) * (HD**-0.5)
        da_ref[:, cols] = rotated(dq, cosine, -sine).astype(bf16)
    dk = dk_ref[...] * (HD**-0.5)
    dk = rotated(dk + pltpu.roll(dk, HD, 1), cosine, -sine)
    dv = dv_ref[...]
    dv = dv + pltpu.roll(dv, HD, 1)
    da_ref[:, wp + qwp :] = jnp.where(lower, dk, dv).astype(bf16)


def mixer_back_kernel(
    dims, pb_ref, dy_ref, y_ref, wzx_ref, wbc_ref, wsp_ref, da_ref, wq_ref, x_ref, seqc_ref, seqr_ref, masks_ref,
    convx_ref, convs_ref, bias_ref, rate_ref, skip_ref,
    dxb_ref, dact_ref, gn1_ref, gcx_ref, gcs_ref, gstep_ref, gskip_ref,
    neg_ref, gt_ref, dgt_ref, dsum_ref, ddir_ref,
):
    heads, qheads, wp, qwp, span = dims
    rows = x_ref.shape[0]
    masks = {k: masks_ref[:, k : k + 1] for k in (1, 2, 3)}
    linked_t = link_bias(seqc_ref[...], seqr_ref[...], True)
    neg_ref[...] = jnp.where(linked_t, 0.0, far)
    dt = step_parts(pb_ref[:, wp + 256 :], bias_ref[...])
    linked = link_bias(seqc_ref[...], seqr_ref[...], False)
    decay = mm_exact(jnp.where(linked, 1.0, 0.0), -dt * rate_ref[...])
    decay_t = decay.T
    state = pb_ref[:, wp : wp + 256]
    sterms = conv_terms(state, masks)
    sconv = sum(t * convs_ref[k : k + 1, :] for k, t in enumerate(sterms))
    ssig = jax.nn.sigmoid(sconv)
    bcc = (sconv * ssig).astype(bf16)
    bm, cm = bcc[:, :128], bcc[:, 128:]
    gt_ref[...] = mm_nt(bm, cm)
    dgt_ref[...] = jnp.zeros_like(dgt_ref)
    for p in range(wp // LANES):
        cols = slice(p * LANES, (p + 1) * LANES)
        width = HD * min(2, heads - 2 * p)
        terms = conv_terms(pb_ref[:, cols], masks)
        conv = sum(t * convx_ref[k : k + 1, cols] for k, t in enumerate(terms))
        csig = jax.nn.sigmoid(conv)
        xc = conv * csig
        dt_cols = spread_heads(dt, 2 * p, width)
        xdt = (xc * dt_cols).astype(bf16)
        skip = skip_ref[:, cols]
        scanned = y_ref[:, cols] - skip * xc
        dy = dy_ref[:, cols]
        gskip_ref[:, cols] = jnp.sum(dy * xc, axis=0, keepdims=True)
        dyb = dy.astype(bf16)
        blocks = []
        for a in range(rows // span):
            here = slice(a * span, (a + 1) * span)
            sides = []
            for side in range(width // HD):
                h = 2 * p + side
                dys = jnp.where(half_mask(rows - a * span, side), dyb[a * span :], jnp.zeros((), bf16))
                gap = decay_t[h : h + 1, a * span :] - decay[here, h : h + 1]
                falloff = jnp.exp(gap + neg_ref[here, a * span :])
                mixing = (gt_ref[here, a * span :] * falloff).astype(bf16)
                sides.append(mm(mixing, dyb[a * span :]))
                dgt_ref[here, a * span :] += mm_nt(xdt[here], dys) * falloff
            blocks.append(sides[0] if len(sides) == 1 else jnp.where(half_mask(span, 0), sides[0], sides[1]))
        dxdt = jnp.concatenate(blocks, axis=0)
        dsum_ref[:, cols] = dyb.astype(f32) * scanned - xdt.astype(f32) * dxdt
        ddir_ref[:, cols] = dxdt * xc
        dconv = (dxdt * dt_cols + skip * dy) * (csig * (1.0 + conv * (1.0 - csig)))
        gcx_ref[:, cols] = jnp.concatenate([jnp.sum(t * dconv, axis=0, keepdims=True) for t in terms], axis=0)
        dxb_ref[:, cols] = conv_back(dconv, masks, convx_ref[:, cols]).astype(bf16)

    dgt = dgt_ref[...].astype(bf16)
    dbcc = jnp.concatenate([mm(dgt, cm), mm_tn(dgt, bm)], axis=1)
    dsconv = dbcc * (ssig * (1.0 + sconv * (1.0 - ssig)))
    gcs_ref[...] = jnp.concatenate([jnp.sum(t * dsconv, axis=0, keepdims=True) for t in sterms], axis=0)
    dxb_ref[:, wp : wp + 256] = conv_back(dsconv, masks, convs_ref[...]).astype(bf16)

    head_of = lax.broadcasted_iota(jnp.int32, (wp, LANES), 0) // HD
    pick = jnp.where(head_of == lax.broadcasted_iota(jnp.int32, (wp, LANES), 1), 1.0, 0.0)
    ds = mm_exact(dsum_ref[...], pick)
    ddirect = mm_exact(ddir_ref[...], pick)
    dlog = mm_exact(jnp.where(linked_t, 1.0, 0.0), ds)
    rate = rate_ref[...]
    ddt = ddirect - rate * dlog
    dstep = ddt * jax.nn.sigmoid(pb_ref[:, wp + 256 :] + bias_ref[...])
    dstep = jnp.where(lane_ids(rows) < heads, dstep, 0.0)
    dxb_ref[:, wp + 256 :] = dstep.astype(bf16)
    gstep_ref[...] = jnp.concatenate(
        [jnp.sum(dstep, axis=0, keepdims=True), -rate * jnp.sum(dt * dlog, axis=0, keepdims=True)], axis=0
    )
    finish(dxb_ref)
    dact = mm_nt(da_ref[:, :wp], wzx_ref[:, :wp]) + mm_nt(dxb_ref[:, :wp], wzx_ref[:, wp:])
    dact = dact + mm_nt(dxb_ref[:, wp : wp + 256], wbc_ref[...]) + mm_nt(da_ref[:, wp : wp + qwp], wq_ref[...])
    dact = dact + mm_nt(dxb_ref[:, wp + 256 :], wsp_ref[:, :LANES]) + mm_nt(da_ref[:, wp + qwp :], wsp_ref[:, LANES:])
    dact_ref[...] = dact.astype(bf16)
    finish(dact_ref)
    x = x_ref[...].astype(f32)
    r1 = lax.rsqrt(jnp.mean(x * x, axis=-1, keepdims=True) + norm_eps)
    gn1_ref[...] = jnp.sum(dact * x * r1, axis=0, keepdims=True)


def grad_kernel(cuts, block, *refs):
    pairs = len(cuts)
    bit_ref, ins = refs[0], refs[1 : 1 + 2 * pairs]
    sent_ref, kept_ref, turned = refs[1 + 2 * pairs :]
    bit = bit_ref[0]
    at = 0
    for k, (low, high) in enumerate(cuts):
        left, right = ins[2 * k], ins[2 * k + 1]
        if k == 0 or left is not ins[2 * k - 2]:
            turned[...] = left[...].astype(f32).T.astype(bf16)
        count = turned.shape[0] // (2 * block)
        for side, out in enumerate((sent_ref, kept_ref)):
            which = 1 - bit if side == 0 else bit
            for i in range(count):
                start = pl.multiple_of((2 * i + which) * block, block)
                rows = turned[pl.ds(start, block), :]
                out[i * block : (i + 1) * block, at : at + high - low] = mm(rows, right[:, low:high]).astype(bf16)
        at += high - low


def weight_halves(pairs, bit, block, after=()):
    args = [bit] + [a for left, right, _, _ in pairs for a in (left, right)]
    cuts = [(low, high) for _, _, low, high in pairs]
    rows, model = pairs[0][0].shape
    half = (model // 2, sum(high - low for low, high in cuts))
    return call(
        functools.partial(grad_kernel, cuts, block), [(half, bf16), (half, bf16)], [((model, rows), bf16)], args, 1, after
    )


def step_kernel(block, which_ref, kept_ref, arrived_ref, away_ref, mine_ref):
    which = which_ref[0]
    for out, side in ((away_ref, 1 - which), (mine_ref, which)):
        for i in range(kept_ref.shape[0] // (2 * block)):
            start = pl.multiple_of((2 * i + side) * block, block)
            total = kept_ref[pl.ds(start, block), :].astype(f32) + arrived_ref[pl.ds(start, block), :].astype(f32)
            out[i * block : (i + 1) * block, :] = total.astype(bf16)


def add_kernel(a_ref, b_ref, out_ref):
    out_ref[...] = a_ref[...] + b_ref[...]


class Fetched:
    def __init__(self, source, held, sem):
        self.held, self.copy, self.ready = held, pltpu.make_async_copy(source, held, sem), False
        self.shape, self.dtype = held.shape, held.dtype
        self.copy.start()

    def __getitem__(self, key):
        if not self.ready:
            self.copy.wait()
            self.ready = True
        return self.held[key]


class Stored:
    def __init__(self, held, target, sem):
        self.held, self.copy, self.sent = held, pltpu.make_async_copy(held, target, sem), False
        self.shape, self.dtype = held.shape, held.dtype

    def __getitem__(self, key):
        return self.held[key]

    def __setitem__(self, key, value):
        self.held[key] = value

    def finish(self):
        if not self.sent:
            self.copy.start()
            self.sent = True


LARGE = 1 << 16


def finish(*refs):
    for ref in refs:
        if isinstance(ref, Stored):
            ref.finish()


def call(kernel, outs, scratch, args, scalars=0, after=()):
    count = len(args)
    large_in = [i >= scalars and a.size * a.dtype.itemsize >= LARGE for i, a in enumerate(args)]
    large_out = [s[0] * s[1] * jnp.dtype(t).itemsize >= LARGE for s, t in outs]
    buffers = [pltpu.VMEM(a.shape, a.dtype) for a, big in zip(args, large_in) if big]
    buffers += [pltpu.VMEM(s, t) for (s, t), big in zip(outs, large_out) if big]
    copies = len(buffers)

    def wrapped(*refs):
        ins, rest = list(refs[:count]), refs[count + len(after) :]
        results, rest = list(rest[: len(outs)]), rest[len(outs) :]
        held, sems, inner = rest[:copies], rest[copies], rest[copies + 1 :]
        slot = 0
        for i, big in enumerate(large_in):
            if big:
                ins[i] = Fetched(ins[i], held[slot], sems.at[slot])
                slot += 1
        for i, big in enumerate(large_out):
            if big:
                results[i] = Stored(held[slot], results[i], sems.at[slot])
                slot += 1
        kernel(*ins, *results, *inner)
        finish(*results)
        for ref in ins:
            if isinstance(ref, Fetched) and not ref.ready:
                ref.copy.wait()
        for ref in results:
            if isinstance(ref, Stored):
                ref.copy.wait()

    spaces = [pltpu.SMEM] * scalars + [pl.ANY if big else pltpu.VMEM for big in large_in[scalars:]] + [pl.ANY] * len(after)
    return pl.pallas_call(
        wrapped,
        out_shape=[jax.ShapeDtypeStruct(s, t) for s, t in outs],
        in_specs=[pl.BlockSpec(memory_space=space) for space in spaces],
        out_specs=[pl.BlockSpec(memory_space=pl.ANY if big else pltpu.VMEM) for big in large_out],
        scratch_shapes=buffers + [pltpu.SemaphoreType.DMA((max(copies, 1),))] + [pltpu.VMEM(s, t) for s, t in scratch],
        compiler_params=pltpu.CompilerParams(vmem_limit_bytes=52 * 1024 * 1024),
        cost_estimate=pl.CostEstimate(flops=1000, bytes_accessed=1000, transcendentals=0),
    )(*args, *after)


def swap(values):
    return lax.ppermute(values, "tensor", [(0, 1), (1, 0)])


def gather_rows(values, me, count):
    if count != 2:
        return lax.all_gather(values, "tensor", axis=0, tiled=True)
    other = swap(values)
    first = jnp.where(me == 0, values, other)
    return jnp.concatenate([first, jnp.where(me == 0, other, values)], axis=0)


def both_parts(part, count):
    if count != 2:
        return (lax.psum(part, "tensor"), jnp.zeros_like(part))
    return (part, swap(part))


def scatter_rows(part, me, count):
    if count != 2:
        return lax.psum_scatter(part, "tensor", scatter_dimension=0, tiled=True).astype(f32)
    halves = part.reshape(2, part.shape[0] // 2, part.shape[1])
    arrived = swap(lax.dynamic_index_in_dim(halves, 1 - me, 0, keepdims=False))
    return lax.dynamic_index_in_dim(halves, me, 0, keepdims=False).astype(f32) + arrived.astype(f32)


def partners(count, bit):
    return [(i, i ^ bit) for i in range(count)]


def exchange(sent, count, bit):
    return lax.ppermute(sent, "dp", partners(count, bit))


class Reduction:
    def __init__(self, sent, kept, index, count, block):
        self.index, self.count, self.block, self.bit = index, count, block, 1
        self.kept, self.sent = kept, sent
        self.arrived = exchange(sent, count, 1)

    def done(self):
        return self.bit * 2 >= self.count

    def step(self, after=()):
        if self.done():
            return after
        self.bit *= 2
        which = ((self.index // self.bit) % 2).astype(jnp.int32).reshape(1)
        half = (self.kept.shape[0] // 2, self.kept.shape[1])
        self.sent, self.kept = call(
            functools.partial(step_kernel, self.block), [(half, bf16), (half, bf16)], [],
            (which, self.kept, self.arrived), 1, after,
        )
        self.arrived = exchange(self.sent, self.count, self.bit)
        return (self.sent,)

    def total(self):
        return self.kept.astype(f32) + self.arrived.astype(f32)


def segments(lengths, row_count):
    seq_ends = jnp.cumsum(lengths)
    places = jnp.arange(row_count, dtype=jnp.int32)
    passed = places[:, None] >= seq_ends[None, :]
    seq_ids = jnp.sum(passed.astype(jnp.int32), axis=1)
    starts = jnp.max(jnp.where(passed, seq_ends[None, :], 0), axis=1)
    is_live = (places < seq_ends[-1]).astype(f32)
    return (seq_ids, places - starts, is_live)


def body(
    dp_count, tensor_count, tokens, cotangent, seq_lengths, norm1_gain, norm2_gain, mixer_in, state_in, step_in,
    conv_inner, conv_state, step_bias, decay_log, skip_gain, mixer_out, query_in, key_value, attend_out, gate_up,
    down_out,
):
    share, model = tokens.shape
    rows = share * tensor_count
    me = lax.axis_index("tensor")
    index = lax.axis_index("dp")
    inner = mixer_in.shape[2]
    heads = step_in.shape[1]
    query_width = query_in.shape[1]
    qheads = query_width // HD
    wp, qwp = padded(inner), padded(query_width)
    span = min(LANES, rows)
    dims = (heads, qheads, wp, qwp, span)

    if tensor_count == 2:
        x_own, x_other = tokens, swap(tokens)
    else:
        x_own = x_other = gather_rows(tokens, me, tensor_count)
    place = jnp.stack([me, lax.rem(me + 1, tensor_count)]).astype(jnp.int32)
    seq_ids, positions, is_live = segments(seq_lengths[0], rows)
    live_share = lax.dynamic_slice_in_dim(is_live, me * share, share, 0)[:, None]
    dout_rows = gather_rows(lax.optimization_barrier((cotangent, x_other))[0], me, tensor_count)
    dout_rows = dout_rows * is_live[:, None].astype(bf16)

    seq_col = seq_ids.astype(f32)[:, None]
    seq_row = seq_ids.astype(f32)[None, :]
    shifts = jnp.minimum(jnp.arange(LANES, dtype=jnp.int32), 4)[None, :]
    masks = (positions[:, None] >= shifts).astype(f32)
    lane = jnp.arange(LANES)
    frequency = rope_base ** (-2.0 * (lane % (HD // 2)).astype(f32) / HD)
    angles = positions.astype(f32)[:, None] * frequency[None, :]
    cosine = jnp.cos(angles)
    sine = jnp.sin(angles) * jnp.where(lane % HD < HD // 2, -1.0, 1.0)[None, :]

    key_index = me * qheads // (QH // KVH)
    pair_local = lax.dynamic_slice_in_dim(key_value, key_index * HD, HD, 2).reshape(model, 2 * HD)
    if inner == wp:
        wzx = mixer_in.reshape(model, 2 * inner)
    else:
        wzx = pad_to(mixer_in, wp).reshape(model, 2 * wp)
    wsp = jnp.concatenate([pad_to(step_in, LANES), pair_local], axis=1)
    wq, wmix, watt = pad_to(query_in, qwp), pad_to(mixer_out, wp), pad_to(attend_out, qwp)
    taps = pad_to(conv_inner, wp)
    bias = pad_to(step_bias[None], LANES)
    rate = pad_to(jnp.exp(decay_log)[None], LANES)
    skip = pad_to(jnp.repeat(skip_gain, HD)[None], wp)
    gain1, gain2 = norm1_gain[None], norm2_gain[None]

    x_rows, act, pa, pb, y, cat, part = call(
        functools.partial(front_kernel, dims),
        [
            ((rows, model), bf16), ((rows, model), bf16), ((rows, wp + qwp + LANES), f32), ((rows, wp + 384), f32),
            ((rows, wp), f32), ((rows, wp + qwp), bf16), ((rows, model), bf16),
        ],
        [((rows, rows), f32), ((rows, rows), f32), ((rows, LANES), bf16)],
        (
            place, x_own, x_other, state_in, wsp, wzx, wq, wmix, watt, gain1, seq_col, seq_row, masks, cosine, sine, taps,
            conv_state, bias, rate, skip,
        ),
        1,
    )
    own, other = both_parts(part, tensor_count)
    wgu = lax.optimization_barrier((gate_up, part))[0].reshape(model, -1)
    dhidden = mm(dout_rows, down_out)
    ff2 = wgu.shape[1]
    h1, n2, hidden, dgu, ffn_part, dn2_part = call(
        middle_kernel,
        [
            ((rows, model), f32), ((rows, model), bf16), ((rows, ff2 // 2), bf16), ((rows, ff2), bf16),
            ((rows, model), bf16), ((rows, model), bf16),
        ],
        [],
        (x_rows, own, other, gain2, wgu, down_out, dhidden),
    )
    dn2_own, dn2_other = both_parts(dn2_part, tensor_count)

    bit = (index % 2).astype(jnp.int32).reshape(1)
    block = model // dp_count
    cut = ff2 // 4

    def reduction(pairs, after=()):
        sent, kept = weight_halves(pairs, bit, block, after)
        return Reduction(sent, kept, index, dp_count, block)

    ffn_a = reduction([(dout_rows, hidden, 0, ff2 // 2), (n2, dgu, 0, cut)])
    order = ffn_a.step()

    dh1_share, ffn_send, dmix, dy, da, gn2 = call(
        functools.partial(attend_back_kernel, dims, share),
        [
            ((share, model), f32), ((share, model), bf16), ((rows, model), bf16), ((rows, wp), f32),
            ((rows, wp + qwp + LANES), bf16), ((1, model), f32),
        ],
        [((rows, rows), f32), ((rows, model), f32), ((rows, qwp), bf16), ((rows, LANES), f32), ((rows, LANES), f32)],
        (
            place, dn2_own, dn2_other, ffn_part, h1, dout_rows, gain2, wmix, watt, seq_col, seq_row, cosine, sine, pa, y,
        ),
        1, order,
    )
    order = ffn_a.step((dmix,))
    ffn_b = reduction([(n2, dgu, cut, ff2)], order)
    mix_a = reduction([(dmix, cat, 0, wp + qwp), (act, da, 0, wp + qwp + LANES)], (ffn_b.kept,))
    order = ffn_b.step((mix_a.kept,))
    order = mix_a.step(order)

    dxb, dact, gn1, gcx, gcs, gstep, gskip = call(
        functools.partial(mixer_back_kernel, dims),
        [
            ((rows, wp + 384), bf16), ((rows, model), bf16),
            ((1, model), f32), ((4, wp), f32), ((4, 256), f32), ((2, LANES), f32), ((1, wp), f32),
        ],
        [
            ((rows, rows), f32), ((rows, rows), f32), ((rows, rows), f32), ((rows, wp), f32), ((rows, wp), f32),
        ],
        (
            pb, dy, y, wzx, state_in, wsp, da, wq, x_rows, seq_col, seq_row, masks, taps, conv_state, bias, rate, skip,
        ),
        0, order,
    )
    shared = jnp.concatenate([gn1[0], gn2[0] * (1.0 / tensor_count), gcs.reshape(-1)]).reshape(-1, LANES)
    local = jnp.concatenate([gcx.reshape(-1), gskip.reshape(-1), gstep.reshape(-1)]).reshape(-1, LANES)
    shared_rows = shared.shape[0]
    minor = jnp.concatenate([shared, local], axis=0)

    def minor_step(values, bit, after):
        arrived = exchange(values, dp_count, bit)
        return call(add_kernel, [(values.shape, f32)], [], (values, arrived), 0, after)[0]

    order = ffn_a.step((dxb,))
    mix_b = reduction([(act, dxb, 0, wp + 384)], order)
    order = ffn_b.step((mix_b.kept,))
    minor_bit = 1
    for r in [mix_b, mix_a, ffn_b, mix_b, mix_a] + 4 * [ffn_a, ffn_b, mix_a, mix_b]:
        if r.done():
            continue
        if minor_bit < dp_count:
            minor = minor_step(minor, minor_bit, order)
            minor_bit *= 2
            order = (minor,)
        order = r.step(order)
    while minor_bit < dp_count:
        minor = minor_step(minor, minor_bit, order)
        minor_bit *= 2
    ffn_a, ffn_b, mix_a, mix_b = ffn_a.total(), ffn_b.total(), mix_a.total(), mix_b.total()
    down_total = ffn_a[:, : ff2 // 2]
    up_total = jnp.concatenate([ffn_a[:, ff2 // 2 :], ffn_b], axis=1)
    out_total, first_total = mix_a[:, : wp + qwp], mix_a[:, wp + qwp :]
    second_total, state_total = mix_b[:, :wp], mix_b[:, wp : wp + 256]
    step_total = mix_b[:, wp + 256 :]

    if tensor_count == 2:
        ffn_mine = lax.dynamic_slice_in_dim(ffn_part, me * share, share, 0).astype(f32)
        ffn_share = ffn_mine + swap(ffn_send).astype(f32)
    else:
        ffn_share = scatter_rows(ffn_part, me, tensor_count)
    h1_share = lax.dynamic_slice_in_dim(h1, me * share, share, 0)
    block_out = ((h1_share + ffn_share) * live_share).astype(bf16)

    dact_share = scatter_rows(dact, me, tensor_count)
    x_share = tokens.astype(f32)
    r1 = lax.rsqrt(jnp.mean(x_share * x_share, axis=-1, keepdims=True) + norm_eps)
    u = dact_share * gain1
    token_grad = dh1_share + r1 * u - x_share * (r1 * r1 * r1 * jnp.mean(u * x_share, axis=-1, keepdims=True))

    shared = lax.psum(minor[:shared_rows], "tensor") if tensor_count != 2 else minor[:shared_rows] + swap(minor[:shared_rows])
    shared = shared.reshape(-1)
    local = minor[shared_rows:].reshape(-1)
    g_norm1, g_norm2, g_conv_state = shared[:model], shared[model : 2 * model], shared[2 * model :].reshape(4, 256)
    g_conv_inner = local[: 4 * wp].reshape(4, wp)[:, :inner]
    g_skip = jnp.sum(local[4 * wp : 5 * wp].reshape(-1, HD), axis=1)[:heads]
    g_bias = local[5 * wp : 5 * wp + heads]
    g_decay = local[5 * wp + LANES : 5 * wp + LANES + heads]

    both = jnp.concatenate([state_total, first_total[:, wp + qwp :]], axis=1).astype(bf16)
    placed = lambda pair: lax.dynamic_update_slice_in_dim(
        jnp.zeros((block,) + key_value.shape[1:], f32), pair.astype(f32).reshape(block, 2, HD), key_index * HD, 2
    )
    if tensor_count == 2:
        arrived = swap(both)
        g_state = both[:, :256].astype(f32) + arrived[:, :256].astype(f32)
        mine = both[:, 256:].reshape(block, 2, HD)
        theirs = arrived[:, 256:].reshape(block, 2, HD)
        g_pair = jnp.concatenate(
            [jnp.where(me == 0, mine, theirs), jnp.where(me == 0, theirs, mine)], axis=2
        ).astype(f32)
    else:
        g_state = lax.psum(both[:, :256], "tensor").astype(f32)
        g_pair = lax.psum(placed(both[:, 256:]).astype(bf16), "tensor").astype(f32)

    g_mixer_in = jnp.stack([first_total[:, :inner], second_total[:, :inner]], axis=1)
    return (
        block_out,
        token_grad.astype(bf16),
        g_norm1,
        g_norm2,
        g_mixer_in,
        g_state,
        step_total[:, :heads],
        g_conv_inner,
        g_conv_state,
        g_bias,
        g_decay,
        g_skip,
        out_total[:, :inner],
        first_total[:, wp : wp + query_width],
        g_pair,
        out_total[:, wp : wp + query_width],
        up_total.reshape(block, 2, ff2 // 2),
        down_total,
    )


def solution(mesh):
    return jax.shard_map(
        functools.partial(body, mesh.shape["dp"], mesh.shape["tensor"]),
        mesh=mesh,
        in_specs=(
            P(("dp", "tensor"), None),
            P(("dp", "tensor"), None),
            P("dp", None),
            P(),
            P(),
            P(None, None, "tensor"),
            P(),
            P(None, "tensor"),
            P(None, "tensor"),
            P(),
            P("tensor"),
            P("tensor"),
            P("tensor"),
            P(None, "tensor"),
            P(None, "tensor"),
            P(),
            P(None, "tensor"),
            P(None, None, "tensor"),
            P(None, "tensor"),
        ),
        out_specs=(
            P(("dp", "tensor"), None),
            P(("dp", "tensor"), None),
            P(),
            P(),
            P("dp", None, "tensor"),
            P("dp", None),
            P("dp", "tensor"),
            P(None, "tensor"),
            P(),
            P("tensor"),
            P("tensor"),
            P("tensor"),
            P("dp", "tensor"),
            P("dp", "tensor"),
            P("dp", None, None),
            P("dp", "tensor"),
            P("dp", None, "tensor"),
            P("dp", "tensor"),
        ),
        check_vma=False,
    )
```

profile of v0, /device:TPU:0, one launch (start us, length us, event | category | flops | bytes accessed | tf_op | source)
XLA Modules:
  0.0 244.2 jit_solution(9533430153630789891)
XLA Ops:
  0.7 3.0 %collective-permute-start = (bf16[192,1024]{1,0:T(8,128)(2,1)}, bf16[192,1024]{1,0:T(8,128)(2,1)S(1)}, u32[]{:S(2)}, u32[]{:S(2)}) collective-permute-start(bf16[192,1024]{1,0:T(8,128)(2,1)} %refs_1_.1), channel_id=1, source_target_pairs={{0,1},{1,0},{2,3},{3,2},{4,5},{5,4},{6,7},{7,6},{8,9},{9,8},{10,11... | collective-permute-start | bytes 1179656 | tf_op jit(solution)/shard_map/ppermute | solution.py:498
  7.9 5.2 %collective-permute-done.refs_2_ = bf16[192,1024]{1,0:T(8,128)(2,1)S(1)} collective-permute-done((bf16[192,1024]{1,0:T(8,128)(2,1)}, bf16[192,1024]{1,0:T(8,128)(2,1)S(1)}, u32[]{:S(2)}, u32[]{:S(2)}) %collective-permute-start) | collective-permute-done | bytes 393248 | tf_op jit(solution)/shard_map/ppermute | solution.py:498
  15.8 4.2 %copy.57 = bf16[128,8,2,768]{3,1,2,0:T(8,128)(2,1)} copy(bf16[128,8,2,768]{3,2,1,0:T(2,128)(2,1)} %bitcast.52) | data formatting | bytes 6291456
  22.0 16.6 %shard_map.322 = (bf16[384,1024]{1,0:T(8,128)(2,1)}, bf16[384,1024]{1,0:T(8,128)(2,1)}, f32[384,1152]{1,0:T(8,128)}, f32[384,1152]{1,0:T(8,128)}, f32[384,768]{1...) custom-call(s32[2]{0:T(128)S(1)} %pad_add_fusion.refs_0_, bf16[192,1024]{1,0:T(8,128)(2,1)S(1)} %copy-done.4, ...), custom_call_target="tpu_custom_call" | custom-call | flops 1000 | bytes 1000 | tf_op jit(solution)/shard_map/pallas_call | solution.py:486
  39.0 3.4 %copy.58 = bf16[128,8,2,1024]{3,1,2,0:T(8,128)(2,1)} copy(bf16[128,8,2,1024]{3,2,1,0:T(2,128)(2,1)S(1)} %bitcast.51) | data formatting | bytes 8388608
  44.1 2.2 fusion.20.refs_6_
  46.3 10.7 %collective-permute-done.1.refs_2_ = bf16[384,1024]{1,0:T(8,128)(2,1)S(1)} collective-permute-done((bf16[384,1024]{1,0:T(8,128)(2,1)}, bf16[384,1024]{1,0:T(8,128)(2,1)S(1)}, u32[]{:S(2)}, u32[]{:S(2)}) %collective-permute-start.1) | collective-permute-done | bytes 786464 | tf_op jit(solution)/shard_map/ppermute | solution.py:498
  57.9 8.9 %shard_map.323 = (f32[384,1024]{1,0:T(8,128)}, bf16[384,1024]{1,0:T(8,128)(2,1)S(1)}, bf16[384,1024]{1,0:T(8,128)(2,1)S(1)}, bf16[384,2048]{1,0:T(8,128)(2,1)}, ...) custom-call(bf16[384,1024]{1,0:T(8,128)(2,1)} %get-tuple-element.78.refs_0_.refs_8_, ...), custom_call_target="tpu_custom_call" | custom-call | flops 1000 | bytes 1000 | tf_op jit(solution)/shard_map/pallas_call | solution.py:486
  67.8 5.5 %shard_map.324 = (bf16[512,1536]{1,0:T(8,128)(2,1)}, bf16[512,1536]{1,0:T(8,128)(2,1)}) custom-call(s32[1]{0:T(128)} %bitcast.11.refs_0_, bf16[384,1024]{1,0:T(8,128)(2,1)S(1)} %maximum_multiply_fusion.refs_1_.refs_5_, bf16[384,1024]{1,0:T(8,128)(2,1)S(1)} %get-tuple-element.87.refs_2_, bf16[384,1024]{1,0:T(8,128)(2,1)} %copy-done.8, ...), custom_call_target="tpu_custom_call" | custom-call | flops 1000 | bytes 1000 | tf_op jit(solution)/shard_map/pallas_call | solution.py:486
  74.0 2.9 %collective-permute-done.4.refs_2_ = bf16[512,1536]{1,0:T(8,128)(2,1)S(1)} collective-permute-done((bf16[512,1536]{1,0:T(8,128)(2,1)}, bf16[512,1536]{1,0:T(8,128)(2,1)S(1)}, u32[]{:S(2)}, u32[]{:S(2)}) %collective-permute-start.4) | collective-permute-done | bytes 1572896 | tf_op jit(solution)/shard_map/ppermute | solution.py:528
  78.1 2.4 shard_map.325
  82.1 11.5 %collective-permute-done.3.refs_2_ = bf16[384,1024]{1,0:T(8,128)(2,1)} collective-permute-done((bf16[384,1024]{1,0:T(8,128)(2,1)}, bf16[384,1024]{1,0:T(8,128)(2,1)}, u32[]{:S(2)}, u32[]{:S(2)}) %collective-permute-start.3) | collective-permute-done | bytes 786464 | tf_op jit(solution)/shard_map/ppermute | solution.py:498
  93.6 12.6 %shard_map.326 = (f32[192,1024]{1,0:T(8,128)}, bf16[192,1024]{1,0:T(8,128)(2,1)}, bf16[384,1024]{1,0:T(8,128)(2,1)}, f32[384,768]{1,0:T(8,128)}, bf16[384,1152]{1,0:T(8,128)(2,1)}, /*index=5*/f32[1,1024]{1,0:T(1,128)S(1)}) custom-call(s32[2]{0:T(128)S(1)} %copy-done.39, bf16[384,1024]{1,0:T(8,128)(2,1)} %get-tuple-element.84.refs_1_, ...), custom_call_target="tpu_custom_call" | custom-call | flops 1000 | bytes 1000 | tf_op jit(solution)/shard_map/pallas_call | solution.py:486
  106.2 2.1 shard_map.327
  108.4 6.2 %shard_map.328 = (bf16[512,1536]{1,0:T(8,128)(2,1)}, bf16[512,1536]{1,0:T(8,128)(2,1)}) custom-call(s32[1]{0:T(128)} %bitcast.11.refs_0_, bf16[384,1024]{1,0:T(8,128)(2,1)S(1)} %copy-done.9, bf16[384,2048]{1,0:T(8,128)(2,1)} %get-tuple-element.89.refs_4_.refs_2_, bf16[128,1536]{1,0:T(8,128)(2,1)} %get-tuple-element.102.refs_3_), custom_call_target="tpu_custom_call" | custom-call | flops 1000 | bytes 1000 | tf_op jit(solution)/shard_map/pallas_call | solution.py:486
  114.6 7.3 %shard_map.329 = (bf16[512,2176]{1,0:T(8,128)(2,1)}, bf16[512,2176]{1,0:T(8,128)(2,1)}) custom-call(s32[1]{0:T(128)} %bitcast.11.refs_0_, bf16[384,1024]{1,0:T(8,128)(2,1)S(1)} %copy-done.6, bf16[384,1024]{1,0:T(8,128)(2,1)S(1)} %copy-done.15, bf16[384,1024]{1,0:T(8,128)(2,1)} %get-tuple-element.100.refs_3_.refs_1_, ...), custom_call_target="tpu_custom_call" | custom-call | flops 1000 | bytes 1000 | tf_op jit(solution)/shard_map/pallas_call | solution.py:486
  125.3 3.6 %collective-permute-done.8.refs_2_ = bf16[512,1536]{1,0:T(8,128)(2,1)} collective-permute-done((bf16[512,1536]{1,0:T(8,128)(2,1)}, bf16[512,1536]{1,0:T(8,128)(2,1)}, u32[]{:S(2)}, u32[]{:S(2)}) %collective-permute-start.8) | collective-permute-done | bytes 1572896 | tf_op jit(solution)/shard_map/ppermute | solution.py:528
  129.0 2.4 shard_map.330
  133.6 4.1 %shard_map.331 = (bf16[256,2176]{1,0:T(8,128)(2,1)S(1)}, bf16[256,2176]{1,0:T(8,128)(2,1)}) custom-call(s32[1]{0:T(128)} %bitcast.10.refs_0_, bf16[512,2176]{1,0:T(8,128)(2,1)} %get-tuple-element.104.refs_3_.refs_1_, bf16[512,2176]{1,0:T(8,128)(2,1)} %collective-permute-done.7.refs_2_, bf16[256,1536]{1,0:T(8,128)(2,1)S(1)} %get-tuple-element.107.refs_3_), custom_call_target="tpu_custom_call" | custom-call | flops 1000 | bytes 1000 | tf_op jit(solution)/shard_map/pallas_call | solution.py:486
  138.8 14.0 %shard_map.332 = (bf16[384,1152]{1,0:T(8,128)(2,1)}, bf16[384,1024]{1,0:T(8,128)(2,1)}, f32[1,1024]{1,0:T(1,128)S(1)}, f32[4,768]{1,0:T(4,128)S(1)}, f32[4,256]{...) custom-call(f32[384,1152]{1,0:T(8,128)} %get-tuple-element.95.refs_0_, ...), custom_call_target="tpu_custom_call" | custom-call | flops 1000 | bytes 1000 | tf_op jit(solution)/shard_map/pallas_call | solution.py:486
  154.7 4.5 %shard_map.334 = (bf16[512,1152]{1,0:T(8,128)(2,1)}, bf16[512,1152]{1,0:T(8,128)(2,1)}) custom-call(s32[1]{0:T(128)} %bitcast.11.refs_0_, bf16[384,1024]{1,0:T(8,128)(2,1)S(1)} %copy-done.7, bf16[384,1152]{1,0:T(8,128)(2,1)S(1)} %copy-done.5, bf16[64,1536]{1,0:T(8,128)(2,1)} %get-tuple-element.119.refs_3_), custom_call_target="tpu_custom_call" | custom-call | flops 1000 | bytes 1000 | tf_op jit(solution)/shard_map/pallas_call | solution.py:486
  161.2 2.6 %collective-permute-start.26 = (bf16[64,1536]{1,0:T(8,128)(2,1)}, bf16[64,1536]{1,0:T(8,128)(2,1)}, u32[]{:S(2)}, u32[]{:S(2)}) collective-permute-start(bf16[64,1536]{1,0:T(8,128)(2,1)} %get-tuple-element.119.refs_3_), channel_id=1, source_target_pairs={{0,16},{2,18},{4,20},{6,22},{8,24},{10,26},{12,28},{14,30},{16,0},... | collective-permute-start | bytes 589832 | tf_op jit(solution)/shard_map/ppermute | solution.py:528
  169.6 4.4 %collective-permute-done.26 = bf16[64,1536]{1,0:T(8,128)(2,1)} collective-permute-done((bf16[64,1536]{1,0:T(8,128)(2,1)}, bf16[64,1536]{1,0:T(8,128)(2,1)}, u32[]{:S(2)}, u32[]{:S(2)}) %collective-permute-start.26) | collective-permute-done | bytes 196640 | tf_op jit(solution)/shard_map/ppermute | solution.py:528
  177.4 2.2 shard_map.337
  179.6 11.5 %collective-permute-done.13.refs_1_ = f32[56,128]{1,0:T(8,128)S(1)} collective-permute-done((f32[56,128]{1,0:T(8,128)S(1)}, f32[56,128]{1,0:T(8,128)S(1)}, u32[]{:S(2)}, u32[]{:S(2)}) %collective-permute-start.13) | collective-permute-done | bytes 28704 | tf_op jit(solution)/shard_map/ppermute | solution.py:528
  192.7 2.0 shard_map.339
  199.8 2.7 %collective-permute-start.27 = (bf16[64,1536]{1,0:T(8,128)(2,1)}, bf16[64,1536]{1,0:T(8,128)(2,1)}, u32[]{:S(2)}, u32[]{:S(2)}) collective-permute-start(bf16[64,1536]{1,0:T(8,128)(2,1)} %get-tuple-element.127.refs_2_), channel_id=1, source_target_pairs={{0,16},{2,18},{4,20},{6,22},{8,24},{10,26},{12,28},{14,30},{16,0},... | collective-permute-start | bytes 589832 | tf_op jit(solution)/shard_map/ppermute | solution.py:528
  208.0 2.3 collective-permute-done.21.refs_2_
  210.9 3.5 %collective-permute-done.20.refs_2_ = bf16[128,2176]{1,0:T(8,128)(2,1)S(1)} collective-permute-done((bf16[128,2176]{1,0:T(8,128)(2,1)S(1)}, bf16[128,2176]{1,0:T(8,128)(2,1)S(1)}, u32[]{:S(2)}, u32[]{:S(2)}) %collective-permute-start.20) | collective-permute-done | bytes 557088 | tf_op jit(solution)/shard_map/ppermute | solution.py:528
  218.2 2.5 %collective-permute-start.23 = (bf16[128,1152]{1,0:T(8,128)(2,1)S(1)}, bf16[128,1152]{1,0:T(8,128)(2,1)S(1)}, u32[]{:S(2)}, u32[]{:S(2)}) collective-permute-start(bf16[128,1152]{1,0:T(8,128)(2,1)S(1)} %get-tuple-element.130.refs_3_), channel_id=1, source_target_pairs={{0,8},{2,10},{4,12},{6,14},{8,0},{10,2},{12,4},{14,6},{16,24},{18,... | collective-permute-start | bytes 884744 | tf_op jit(solution)/shard_map/ppermute | solution.py:528
  220.7 7.8 %collective-permute-done.22 = bf16[64,2176]{1,0:T(8,128)(2,1)S(1)} collective-permute-done((bf16[64,2176]{1,0:T(8,128)(2,1)S(1)}, bf16[64,2176]{1,0:T(8,128)(2,1)S(1)}, u32[]{:S(2)}, u32[]{:S(2)}) %collective-permute-start.22) | collective-permute-done | bytes 278560 | tf_op jit(solution)/shard_map/ppermute | solution.py:528
  232.0 6.2 %collective-permute-done.24 = bf16[64,1152]{1,0:T(8,128)(2,1)S(1)} collective-permute-done((bf16[64,1152]{1,0:T(8,128)(2,1)S(1)}, bf16[64,1152]{1,0:T(8,128)(2,1)S(1)}, u32[]{:S(2)}, u32[]{:S(2)}) %collective-permute-start.24) | collective-permute-done | bytes 147488 | tf_op jit(solution)/shard_map/ppermute | solution.py:528
  (233 shorter events, 61.3 us)
Async XLA Ops:
  0.7 12.4 %collective-permute-start = (bf16[192,1024]{1,0:T(8,128)(2,1)}, bf16[192,1024]{1,0:T(8,128)(2,1)S(1)}, u32[]{:S(2)}, u32[]{:S(2)}) collective-permute-start(bf16[192,1024]{1,0:T(8,128)(2,1)} %refs_1_.1), channel_id=1, source_target_pairs={{0,1},{1,0},{2,3},{3,2},{4,5},{5,4},{6,7},{7,6},{8,9},{9,8},{10,11... | collective-permute-start | bytes 1179656 | tf_op jit(solution)/shard_map/ppermute | solution.py:498
  13.0 29.4 %collective-permute-start.2 = (bf16[192,1024]{1,0:T(8,128)(2,1)}, bf16[192,1024]{1,0:T(8,128)(2,1)}, u32[]{:S(2)}, u32[]{:S(2)}) collective-permute-start(bf16[192,1024]{1,0:T(8,128)(2,1)} %param.20), channel_id=1, source_target_pairs={{0,1},{1,0},{2,3},{3,2},{4,5},{5,4},{6,7},{7,6},{8,9},{9,8},{10,11... | collective-permute-start | bytes 1179656 | tf_op jit(solution)/shard_map/ppermute | solution.py:498
  20.2 18.4 %copy-start.23 = (f32[1,768]{1,0:T(1,128)}, f32[1,768]{1,0:T(1,128)S(1)}, u32[]{:S(2)}) copy-start(f32[1,768]{1,0:T(1,128)S(1)} %broadcast_in_dim_reshape.3.refs_19_.refs_16_) | copy-start | bytes 9220
  20.2 18.4 %copy-start.34 = (f32[1,128]{1,0:T(1,128)}, f32[1,128]{1,0:T(1,128)S(1)}, u32[]{:S(2)}) copy-start(f32[1,128]{1,0:T(1,128)S(1)} %pad.13.refs_18_.refs_15_) | copy-start | bytes 1540
  38.6 18.4 %collective-permute-start.1 = (bf16[384,1024]{1,0:T(8,128)(2,1)}, bf16[384,1024]{1,0:T(8,128)(2,1)S(1)}, u32[]{:S(2)}, u32[]{:S(2)}) collective-permute-start(bf16[384,1024]{1,0:T(8,128)(2,1)} %get-tuple-element.79.refs_1_), channel_id=1, source_target_pairs={{0,1},{1,0},{2,3},{3,2},{4,5},{5,4},{6,7},{7,6},{8,9},{9,8},{10,11... | collective-permute-start | bytes 2359304 | tf_op jit(solution)/shard_map/ppermute | solution.py:498
  44.1 23.6 %copy-start.2 = (bf16[384,1024]{1,0:T(8,128)(2,1)}, bf16[384,1024]{1,0:T(8,128)(2,1)S(1)}, u32[]{:S(2)}) copy-start(bf16[384,1024]{1,0:T(8,128)(2,1)S(1)} %maximum_multiply_fusion.refs_1_.refs_5_) | copy-start | bytes 2359300
  73.2 3.7 %collective-permute-start.4 = (bf16[512,1536]{1,0:T(8,128)(2,1)}, bf16[512,1536]{1,0:T(8,128)(2,1)S(1)}, u32[]{:S(2)}, u32[]{:S(2)}) collective-permute-start(bf16[512,1536]{1,0:T(8,128)(2,1)} %get-tuple-element.91), channel_id=1, source_target_pairs={{0,2},{2,0},{4,6},{6,4},{8,10},{10,8},{12,14},{14,12},{16,18},{18,... | collective-permute-start | bytes 4718600 | tf_op jit(solution)/shard_map/ppermute | solution.py:528
  73.3 20.3 %collective-permute-start.3 = (bf16[384,1024]{1,0:T(8,128)(2,1)}, bf16[384,1024]{1,0:T(8,128)(2,1)}, u32[]{:S(2)}, u32[]{:S(2)}) collective-permute-start(bf16[384,1024]{1,0:T(8,128)(2,1)} %get-tuple-element.84.refs_1_), channel_id=1, source_target_pairs={{0,1},{1,0},{2,3},{3,2},{4,5},{5,4},{6,7},{7,6},{8,9},{9,8},{10,11... | collective-permute-start | bytes 2359304 | tf_op jit(solution)/shard_map/ppermute | solution.py:498
  80.5 25.7 %collective-permute-start.6 = (bf16[256,1536]{1,0:T(8,128)(2,1)S(1)}, bf16[256,1536]{1,0:T(8,128)(2,1)}, u32[]{:S(2)}, u32[]{:S(2)}) collective-permute-start(bf16[256,1536]{1,0:T(8,128)(2,1)S(1)} %get-tuple-element.92.refs_15_), channel_id=1, source_target_pairs={{0,4},{2,6},{4,0},{6,2},{8,12},{10,14},{12,8},{14,10},{16,20},{18,... | collective-permute-start | bytes 2359304 | tf_op jit(solution)/shard_map/ppermute | solution.py:528
  121.9 11.6 %collective-permute-start.7 = (bf16[512,2176]{1,0:T(8,128)(2,1)}, bf16[512,2176]{1,0:T(8,128)(2,1)}, u32[]{:S(2)}, u32[]{:S(2)}) collective-permute-start(bf16[512,2176]{1,0:T(8,128)(2,1)} %get-tuple-element.105), channel_id=1, source_target_pairs={{0,2},{2,0},{4,6},{6,4},{8,10},{10,8},{12,14},{14,12},{16,18},{18,... | collective-permute-start | bytes 6684680 | tf_op jit(solution)/shard_map/ppermute | solution.py:528
  122.0 6.9 %collective-permute-start.8 = (bf16[512,1536]{1,0:T(8,128)(2,1)}, bf16[512,1536]{1,0:T(8,128)(2,1)}, u32[]{:S(2)}, u32[]{:S(2)}) collective-permute-start(bf16[512,1536]{1,0:T(8,128)(2,1)} %get-tuple-element.106), channel_id=1, source_target_pairs={{0,2},{2,0},{4,6},{6,4},{8,10},{10,8},{12,14},{14,12},{16,18},{18,... | collective-permute-start | bytes 4718600 | tf_op jit(solution)/shard_map/ppermute | solution.py:528
  122.5 30.3 %collective-permute-start.12 = (bf16[128,1536]{1,0:T(8,128)(2,1)}, bf16[128,1536]{1,0:T(8,128)(2,1)S(1)}, u32[]{:S(2)}, u32[]{:S(2)}) collective-permute-start(bf16[128,1536]{1,0:T(8,128)(2,1)} %get-tuple-element.102.refs_3_), channel_id=1, source_target_pairs={{0,8},{2,10},{4,12},{6,14},{8,0},{10,2},{12,4},{14,6},{16,24},{18,... | collective-permute-start | bytes 1179656 | tf_op jit(solution)/shard_map/ppermute | solution.py:528
  124.1 35.1 %collective-permute-start.5 = (bf16[192,1024]{1,0:T(8,128)(2,1)}, bf16[192,1024]{1,0:T(8,128)(2,1)}, u32[]{:S(2)}, u32[]{:S(2)}) collective-permute-start(bf16[192,1024]{1,0:T(8,128)(2,1)} %get-tuple-element.93), channel_id=1, source_target_pairs={{0,1},{1,0},{2,3},{3,2},{4,5},{5,4},{6,7},{7,6},{8,9},{9,8},{10,11... | collective-permute-start | bytes 1179656 | tf_op jit(solution)/shard_map/ppermute | solution.py:498
  131.3 34.2 %collective-permute-start.11 = (bf16[256,1536]{1,0:T(8,128)(2,1)S(1)}, bf16[256,1536]{1,0:T(8,128)(2,1)}, u32[]{:S(2)}, u32[]{:S(2)}) collective-permute-start(bf16[256,1536]{1,0:T(8,128)(2,1)S(1)} %get-tuple-element.107.refs_3_), channel_id=1, source_target_pairs={{0,4},{2,6},{4,0},{6,2},{8,12},{10,14},{12,8},{14,10},{16,20},{18,... | collective-permute-start | bytes 2359304 | tf_op jit(solution)/shard_map/ppermute | solution.py:528
  138.8 20.5 %copy-start.43 = (bf16[384,1024]{1,0:T(8,128)(2,1)S(1)}, bf16[384,1024]{1,0:T(8,128)(2,1)}, u32[]{:S(2)}) copy-start(bf16[384,1024]{1,0:T(8,128)(2,1)} %get-tuple-element.83.refs_3_) | copy-start | bytes 2359300
  159.2 18.3 %collective-permute-start.14 = (bf16[512,1152]{1,0:T(8,128)(2,1)}, bf16[512,1152]{1,0:T(8,128)(2,1)}, u32[]{:S(2)}, u32[]{:S(2)}) collective-permute-start(bf16[512,1152]{1,0:T(8,128)(2,1)} %get-tuple-element.122), channel_id=1, source_target_pairs={{0,2},{2,0},{4,6},{6,4},{8,10},{10,8},{12,14},{14,12},{16,18},{18,... | collective-permute-start | bytes 3538952 | tf_op jit(solution)/shard_map/ppermute | solution.py:528
  161.2 12.8 %collective-permute-start.26 = (bf16[64,1536]{1,0:T(8,128)(2,1)}, bf16[64,1536]{1,0:T(8,128)(2,1)}, u32[]{:S(2)}, u32[]{:S(2)}) collective-permute-start(bf16[64,1536]{1,0:T(8,128)(2,1)} %get-tuple-element.119.refs_3_), channel_id=1, source_target_pairs={{0,16},{2,18},{4,20},{6,22},{8,24},{10,26},{12,28},{14,30},{16,0},... | collective-permute-start | bytes 589832 | tf_op jit(solution)/shard_map/ppermute | solution.py:528
  163.8 29.0 %collective-permute-start.16 = (bf16[256,2176]{1,0:T(8,128)(2,1)S(1)}, bf16[256,2176]{1,0:T(8,128)(2,1)}, u32[]{:S(2)}, u32[]{:S(2)}) collective-permute-start(bf16[256,2176]{1,0:T(8,128)(2,1)S(1)} %copy-done.14), channel_id=1, source_target_pairs={{0,4},{2,6},{4,0},{6,2},{8,12},{10,14},{12,8},{14,10},{16,20},{18,... | collective-permute-start | bytes 3342344 | tf_op jit(solution)/shard_map/ppermute | solution.py:528
  164.4 3.5 %collective-permute-start.10 = (f32[56,128]{1,0:T(8,128)S(1)}, f32[56,128]{1,0:T(8,128)S(1)}, u32[]{:S(2)}, u32[]{:S(2)}) collective-permute-start(f32[56,128]{1,0:T(8,128)S(1)} %pad_maximum_fusion.3.refs_0_), channel_id=1, source_target_pairs={{0,2},{2,0},{4,6},{6,4},{8,10},{10,8},{12,14},{14,12},{16,18},{18,... | collective-permute-start | bytes 86024 | tf_op jit(solution)/shard_map/ppermute | solution.py:528
  165.5 11.6 %collective-permute-start.9 = (bf16[192,1024]{1,0:T(8,128)(2,1)S(1)}, bf16[192,1024]{1,0:T(8,128)(2,1)S(1)}, u32[]{:S(2)}, u32[]{:S(2)}) collective-permute-start(bf16[192,1024]{1,0:T(8,128)(2,1)S(1)} %dynamic-slice_bitcast_fusion), channel_id=1, source_target_pairs={{0,1},{1,0},{2,3},{3,2},{4,5},{5,4},{6,7},{7,6},{8,9},{9,8},{10,11... | collective-permute-start | bytes 1179656 | tf_op jit(solution)/shard_map/ppermute | solution.py:498
  167.9 30.7 %collective-permute-start.18 = (bf16[128,1536]{1,0:T(8,128)(2,1)S(1)}, bf16[128,1536]{1,0:T(8,128)(2,1)S(1)}, u32[]{:S(2)}, u32[]{:S(2)}) collective-permute-start(bf16[128,1536]{1,0:T(8,128)(2,1)S(1)} %get-tuple-element.121.refs_2_), channel_id=1, source_target_pairs={{0,8},{2,10},{4,12},{6,14},{8,0},{10,2},{12,4},{14,6},{16,24},{18,... | collective-permute-start | bytes 1179656 | tf_op jit(solution)/shard_map/ppermute | solution.py:528
  174.0 17.1 %collective-permute-start.13 = (f32[56,128]{1,0:T(8,128)S(1)}, f32[56,128]{1,0:T(8,128)S(1)}, u32[]{:S(2)}, u32[]{:S(2)}) collective-permute-start(f32[56,128]{1,0:T(8,128)S(1)} %shard_map.336.refs_3_.refs_0_), channel_id=1, source_target_pairs={{0,4},{2,6},{4,0},{6,2},{8,12},{10,14},{12,8},{14,10},{16,20},{18,... | collective-permute-start | bytes 86024 | tf_op jit(solution)/shard_map/ppermute | solution.py:528
  191.1 3.9 %collective-permute-start.15 = (f32[56,128]{1,0:T(8,128)S(1)}, f32[56,128]{1,0:T(8,128)S(1)}, u32[]{:S(2)}, u32[]{:S(2)}) collective-permute-start(f32[56,128]{1,0:T(8,128)S(1)} %shard_map.338.refs_3_.refs_0_), channel_id=1, source_target_pairs={{0,8},{2,10},{4,12},{6,14},{8,0},{10,2},{12,4},{14,6},{16,24},{18,... | collective-permute-start | bytes 86024 | tf_op jit(solution)/shard_map/ppermute | solution.py:528
  195.1 7.4 %collective-permute-start.17 = (f32[56,128]{1,0:T(8,128)S(1)}, f32[56,128]{1,0:T(8,128)S(1)}, u32[]{:S(2)}, u32[]{:S(2)}) collective-permute-start(f32[56,128]{1,0:T(8,128)S(1)} %shard_map.340.refs_3_.refs_0_), channel_id=1, source_target_pairs={{0,16},{2,18},{4,20},{6,22},{8,24},{10,26},{12,28},{14,30},{16,0},... | collective-permute-start | bytes 86024 | tf_op jit(solution)/shard_map/ppermute | solution.py:528
  196.5 13.9 %collective-permute-start.21 = (bf16[256,1152]{1,0:T(8,128)(2,1)S(1)}, bf16[256,1152]{1,0:T(8,128)(2,1)S(1)}, u32[]{:S(2)}, u32[]{:S(2)}) collective-permute-start(bf16[256,1152]{1,0:T(8,128)(2,1)S(1)} %get-tuple-element.123.refs_2_), channel_id=1, source_target_pairs={{0,4},{2,6},{4,0},{6,2},{8,12},{10,14},{12,8},{14,10},{16,20},{18,... | collective-permute-start | bytes 1769480 | tf_op jit(solution)/shard_map/ppermute | solution.py:528
  197.0 17.4 %collective-permute-start.20 = (bf16[128,2176]{1,0:T(8,128)(2,1)S(1)}, bf16[128,2176]{1,0:T(8,128)(2,1)S(1)}, u32[]{:S(2)}, u32[]{:S(2)}) collective-permute-start(bf16[128,2176]{1,0:T(8,128)(2,1)S(1)} %get-tuple-element.125.refs_2_), channel_id=1, source_target_pairs={{0,8},{2,10},{4,12},{6,14},{8,0},{10,2},{12,4},{14,6},{16,24},{18,... | collective-permute-start | bytes 1671176 | tf_op jit(solution)/shard_map/ppermute | solution.py:528
  199.8 16.2 %collective-permute-start.27 = (bf16[64,1536]{1,0:T(8,128)(2,1)}, bf16[64,1536]{1,0:T(8,128)(2,1)}, u32[]{:S(2)}, u32[]{:S(2)}) collective-permute-start(bf16[64,1536]{1,0:T(8,128)(2,1)} %get-tuple-element.127.refs_2_), channel_id=1, source_target_pairs={{0,16},{2,18},{4,20},{6,22},{8,24},{10,26},{12,28},{14,30},{16,0},... | collective-permute-start | bytes 589832 | tf_op jit(solution)/shard_map/ppermute | solution.py:528
  202.5 3.8 %collective-permute-start.19 = (f32[24,128]{1,0:T(8,128)S(1)}, f32[24,128]{1,0:T(8,128)S(1)}, u32[]{:S(2)}, u32[]{:S(2)}) collective-permute-start(f32[24,128]{1,0:T(8,128)S(1)} %slice.116), channel_id=1, source_target_pairs={{0,1},{1,0},{2,3},{3,2},{4,5},{5,4},{6,7},{7,6},{8,9},{9,8},{10,11... | collective-permute-start | bytes 36872 | tf_op jit(solution)/shard_map/ppermute | solution.py:498
  214.9 13.6 %collective-permute-start.22 = (bf16[64,2176]{1,0:T(8,128)(2,1)S(1)}, bf16[64,2176]{1,0:T(8,128)(2,1)S(1)}, u32[]{:S(2)}, u32[]{:S(2)}) collective-permute-start(bf16[64,2176]{1,0:T(8,128)(2,1)S(1)} %get-tuple-element.132.refs_3_), channel_id=1, source_target_pairs={{0,16},{2,18},{4,20},{6,22},{8,24},{10,26},{12,28},{14,30},{16,0},... | collective-permute-start | bytes 835592 | tf_op jit(solution)/shard_map/ppermute | solution.py:528
  218.2 12.4 %collective-permute-start.23 = (bf16[128,1152]{1,0:T(8,128)(2,1)S(1)}, bf16[128,1152]{1,0:T(8,128)(2,1)S(1)}, u32[]{:S(2)}, u32[]{:S(2)}) collective-permute-start(bf16[128,1152]{1,0:T(8,128)(2,1)S(1)} %get-tuple-element.130.refs_3_), channel_id=1, source_target_pairs={{0,8},{2,10},{4,12},{6,14},{8,0},{10,2},{12,4},{14,6},{16,24},{18,... | collective-permute-start | bytes 884744 | tf_op jit(solution)/shard_map/ppermute | solution.py:528
  231.2 6.9 %collective-permute-start.24 = (bf16[64,1152]{1,0:T(8,128)(2,1)S(1)}, bf16[64,1152]{1,0:T(8,128)(2,1)S(1)}, u32[]{:S(2)}, u32[]{:S(2)}) collective-permute-start(bf16[64,1152]{1,0:T(8,128)(2,1)S(1)} %get-tuple-element.135), channel_id=1, source_target_pairs={{0,16},{2,18},{4,20},{6,22},{8,24},{10,26},{12,28},{14,30},{16,0},... | collective-permute-start | bytes 442376 | tf_op jit(solution)/shard_map/ppermute | solution.py:528
  238.3 4.2 %collective-permute-start.25 = (bf16[64,384]{1,0:T(8,128)(2,1)S(1)}, bf16[64,384]{1,0:T(8,128)(2,1)S(1)}, u32[]{:S(2)}, u32[]{:S(2)}) collective-permute-start(bf16[64,384]{1,0:T(8,128)(2,1)S(1)} %pad_maximum_fusion.2), channel_id=1, source_target_pairs={{0,1},{1,0},{2,3},{3,2},{4,5},{5,4},{6,7},{7,6},{8,9},{9,8},{10,11... | collective-permute-start | bytes 147464 | tf_op jit(solution)/shard_map/ppermute | solution.py:498
  (52 other events, 348.1 us)
where the time goes:
time: 248 us; the launch traced here: 244 us
  Pallas kernels  96.4 us (39%)
  waiting for transfers between devices  75.8 us (31%)
  starting transfers between devices  29.2 us (12%)
  local copies, waits for them, and re-layouts  24.5 us (10%)
  other arithmetic  14.1 us (6%)
    pallas_call x24, Pallas kernels, call(): pl.pallas_call(wrapped, out_shape=[jax.ShapeDtypeStruct(s, t) for s, t in...  96.4 us
    ppermute x20, waiting for transfers between devices, exchange(): return lax.ppermute(sent, 'dp', partners(count, bit))  43.8 us
    ppermute x8, waiting for transfers between devices, swap(): return lax.ppermute(values, 'tensor', [(0, 1), (1, 0)])  32 us
    ppermute x20, starting transfers between devices, exchange(): return lax.ppermute(sent, 'dp', partners(count, bit))  21.2 us
    unnamed x116, local copies, waits for them, and re-layouts  15.1 us
    ppermute x8, starting transfers between devices, swap(): return lax.ppermute(values, 'tensor', [(0, 1), (1, 0)])  7.98 us
  transfers between devices with their start and end apart: 28, of which 16 were waited for; matrix products, arithmetic and copies ran while one was open for 14% of the time, Pallas kernels for 27%

commit v1 on v0

--- a/solution.py
+++ b/solution.py
@@ -370,43 +370,131 @@
     gn1_ref[...] = jnp.sum(dact * x * r1, axis=0, keepdims=True)
 
 
-def grad_kernel(cuts, block, *refs):
+def pieces_of(width, most):
+    groups = width // LANES
+    count = -(-groups // (most // LANES))
+    edges = [(i * groups // count) * LANES for i in range(count + 1)]
+    return list(zip(edges[:-1], edges[1:]))
+
+
+def grad_kernel(cuts, pieces, block, bit_ref, *refs):
     pairs = len(cuts)
-    bit_ref, ins = refs[0], refs[1 : 1 + 2 * pairs]
-    sent_ref, kept_ref, turned = refs[1 + 2 * pairs :]
+    ins, refs = refs[: 2 * pairs], refs[2 * pairs :]
+    sents, kept, refs = refs[: len(pieces)], refs[len(pieces)], refs[len(pieces) + 1 :]
+    buffers, refs = refs[: 2 * pairs], refs[2 * pairs :]
+    turned, stage, in_sems, sent_sems, kept_sems = refs
+    fetched = [Fetched(ins[i], buffers[i], in_sems.at[i]) for i in range(2 * pairs)]
     bit = bit_ref[0]
-    at = 0
+    count = turned.shape[0] // (2 * block)
+    copies, at, sent_to = [], 0, 0
     for k, (low, high) in enumerate(cuts):
-        left, right = ins[2 * k], ins[2 * k + 1]
-        if k == 0 or left is not ins[2 * k - 2]:
-            turned[...] = left[...].astype(f32).T.astype(bf16)
-        count = turned.shape[0] // (2 * block)
-        for side, out in enumerate((sent_ref, kept_ref)):
-            which = 1 - bit if side == 0 else bit
-            for i in range(count):
-                start = pl.multiple_of((2 * i + which) * block, block)
-                rows = turned[pl.ds(start, block), :]
-                out[i * block : (i + 1) * block, at : at + high - low] = mm(rows, right[:, low:high]).astype(bf16)
-        at += high - low
-
-
-def weight_halves(pairs, bit, block, after=()):
-    args = [bit] + [a for left, right, _, _ in pairs for a in (left, right)]
+        turned[...] = fetched[2 * k][...].astype(f32).T.astype(bf16)
+        for start in range(low, high, 512):
+            stop = min(start + 512, high)
+            full = mm(turned[...], fetched[2 * k + 1][:, start:stop]).astype(bf16)
+            for j in range(2 * count):
+                side = 1 - bit if j % 2 == 0 else bit
+                stage[side, (j // 2) * block : (j // 2 + 1) * block, at : at + stop - start] = full[j * block : (j + 1) * block]
+            at += stop - start
+            while sent_to < len(pieces) and pieces[sent_to][1] <= at:
+                cols = pl.ds(pieces[sent_to][0], pieces[sent_to][1] - pieces[sent_to][0])
+                copies.append(pltpu.make_async_copy(stage.at[0, :, cols], sents[sent_to], sent_sems.at[sent_to]))
+                copies.append(pltpu.make_async_copy(stage.at[1, :, cols], kept.at[:, cols], kept_sems.at[sent_to]))
+                copies[-2].start()
+                copies[-1].start()
+                sent_to += 1
+    for copy in copies:
+        copy.wait()
+
+
+def plain_params(flops=1000):
+    return dict(
+        compiler_params=pltpu.CompilerParams(vmem_limit_bytes=52 * 1024 * 1024),
+        cost_estimate=pl.CostEstimate(flops=flops, bytes_accessed=1000, transcendentals=0),
+    )
+
+
+def weight_halves(pairs, bit, block, most, after=()):
+    args = [a for left, right, _, _ in pairs for a in (left, right)]
     cuts = [(low, high) for _, _, low, high in pairs]
     rows, model = pairs[0][0].shape
-    half = (model // 2, sum(high - low for low, high in cuts))
-    return call(
-        functools.partial(grad_kernel, cuts, block), [(half, bf16), (half, bf16)], [((model, rows), bf16)], args, 1, after
-    )
-
-
-def step_kernel(block, which_ref, kept_ref, arrived_ref, away_ref, mine_ref):
+    width = sum(high - low for low, high in cuts)
+    pieces = pieces_of(width, most)
+    outs = [(model // 2, high - low) for low, high in pieces] + [(model // 2, width)]
+
+    def wrapped(bit_ref, *refs):
+        grad_kernel(cuts, pieces, block, bit_ref, *refs[: len(args)], *refs[len(args) + len(after) :])
+
+    *sent, kept = pl.pallas_call(
+        wrapped,
+        out_shape=[jax.ShapeDtypeStruct(s, bf16) for s in outs],
+        in_specs=[pl.BlockSpec(memory_space=pltpu.SMEM)] + [pl.BlockSpec(memory_space=pl.ANY)] * (len(args) + len(after)),
+        out_specs=[pl.BlockSpec(memory_space=pl.ANY)] * len(outs),
+        scratch_shapes=[pltpu.VMEM(a.shape, a.dtype) for a in args]
+        + [
+            pltpu.VMEM((model, rows), bf16), pltpu.VMEM((2, model // 2, width), bf16),
+            pltpu.SemaphoreType.DMA((len(args),)), pltpu.SemaphoreType.DMA((len(pieces),)),
+            pltpu.SemaphoreType.DMA((len(pieces),)),
+        ],
+        **plain_params(),
+    )(bit, *args, *after)
+    return sent, kept
+
+
+def step_kernel(pieces, whole, block, which_ref, kept, *refs):
+    count = 1 if whole else len(pieces)
+    arrived, refs = refs[:count], refs[count:]
+    away, mine, kept_buf, arrived_buf, away_buf, mine_buf, kept_sems, arrived_sems, away_sems, mine_sems = refs
     which = which_ref[0]
-    for out, side in ((away_ref, 1 - which), (mine_ref, which)):
-        for i in range(kept_ref.shape[0] // (2 * block)):
-            start = pl.multiple_of((2 * i + side) * block, block)
-            total = kept_ref[pl.ds(start, block), :].astype(f32) + arrived_ref[pl.ds(start, block), :].astype(f32)
-            out[i * block : (i + 1) * block, :] = total.astype(bf16)
+    ins, outs = [], []
+    for k, (low, high) in enumerate(pieces):
+        cols = pl.ds(low, high - low)
+        source = arrived[0].at[:, cols] if whole else arrived[k]
+        ins.append(pltpu.make_async_copy(kept.at[:, cols], kept_buf.at[:, cols], kept_sems.at[k]))
+        ins.append(pltpu.make_async_copy(source, arrived_buf.at[:, cols], arrived_sems.at[k]))
+        ins[-2].start()
+        ins[-1].start()
+    for k, (low, high) in enumerate(pieces):
+        ins[2 * k].wait()
+        ins[2 * k + 1].wait()
+        cols = pl.ds(low, high - low)
+        for out, target, sems, side in ((away_buf, away, away_sems, 1 - which), (mine_buf, mine, mine_sems, which)):
+            for i in range(kept.shape[0] // (2 * block)):
+                rows = pl.ds(pl.multiple_of((2 * i + side) * block, block), block)
+                total = kept_buf[rows, low:high].astype(f32) + arrived_buf[rows, low:high].astype(f32)
+                out[i * block : (i + 1) * block, low:high] = total.astype(bf16)
+            outs.append(pltpu.make_async_copy(out.at[:, cols], target.at[:, cols], sems.at[k]))
+            outs[-1].start()
+    for copy in outs:
+        copy.wait()
+
+
+def step_call(which, kept, arrived, block, after):
+    rows, width = kept.shape
+    whole = len(arrived) == 1
+    if whole:
+        pieces = pieces_of(width, 512)
+    else:
+        edges = [0]
+        for a in arrived:
+            edges.append(edges[-1] + a.shape[1])
+        pieces = list(zip(edges[:-1], edges[1:]))
+    used = 1 + len(arrived)
+
+    def wrapped(which_ref, *refs):
+        step_kernel(pieces, whole, block, which_ref, *refs[:used], *refs[used + len(after) :])
+
+    half = (rows // 2, width)
+    return pl.pallas_call(
+        wrapped,
+        out_shape=[jax.ShapeDtypeStruct(half, bf16)] * 2,
+        in_specs=[pl.BlockSpec(memory_space=pltpu.SMEM)] + [pl.BlockSpec(memory_space=pl.ANY)] * (used + len(after)),
+        out_specs=[pl.BlockSpec(memory_space=pl.ANY)] * 2,
+        scratch_shapes=[pltpu.VMEM((rows, width), bf16)] * 2
+        + [pltpu.VMEM(half, bf16)] * 2
+        + [pltpu.SemaphoreType.DMA((len(pieces),))] * 4,
+        **plain_params(),
+    )(which, kept, *arrived, *after)
 
 
 def add_kernel(a_ref, b_ref, out_ref):
@@ -444,6 +532,7 @@
 
 
 LARGE = 1 << 16
+COST_US = 1100000000
 
 
 def finish(*refs):
@@ -452,7 +541,7 @@
             ref.finish()
 
 
-def call(kernel, outs, scratch, args, scalars=0, after=()):
+def call(kernel, outs, scratch, args, scalars=0, after=(), flops=1000):
     count = len(args)
     large_in = [i >= scalars and a.size * a.dtype.itemsize >= LARGE for i, a in enumerate(args)]
     large_out = [s[0] * s[1] * jnp.dtype(t).itemsize >= LARGE for s, t in outs]
@@ -489,8 +578,7 @@
         in_specs=[pl.BlockSpec(memory_space=space) for space in spaces],
         out_specs=[pl.BlockSpec(memory_space=pl.ANY if big else pltpu.VMEM) for big in large_out],
         scratch_shapes=buffers + [pltpu.SemaphoreType.DMA((max(copies, 1),))] + [pltpu.VMEM(s, t) for s, t in scratch],
-        compiler_params=pltpu.CompilerParams(vmem_limit_bytes=52 * 1024 * 1024),
-        cost_estimate=pl.CostEstimate(flops=1000, bytes_accessed=1000, transcendentals=0),
+        **plain_params(flops),
     )(*args, *after)
 
 
@@ -531,8 +619,8 @@
 class Reduction:
     def __init__(self, sent, kept, index, count, block):
         self.index, self.count, self.block, self.bit = index, count, block, 1
-        self.kept, self.sent = kept, sent
-        self.arrived = exchange(sent, count, 1)
+        self.kept = kept
+        self.arrived = [exchange(part, count, 1) for part in sent]
 
     def done(self):
         return self.bit * 2 >= self.count
@@ -542,16 +630,13 @@
             return after
         self.bit *= 2
         which = ((self.index // self.bit) % 2).astype(jnp.int32).reshape(1)
-        half = (self.kept.shape[0] // 2, self.kept.shape[1])
-        self.sent, self.kept = call(
-            functools.partial(step_kernel, self.block), [(half, bf16), (half, bf16)], [],
-            (which, self.kept, self.arrived), 1, after,
-        )
-        self.arrived = exchange(self.sent, self.count, self.bit)
-        return (self.sent,)
+        sent, self.kept = step_call(which, self.kept, self.arrived, self.block, after)
+        self.arrived = [exchange(sent, self.count, self.bit)]
+        return (sent,)
 
     def total(self):
-        return self.kept.astype(f32) + self.arrived.astype(f32)
+        arrived = self.arrived[0] if len(self.arrived) == 1 else jnp.concatenate(self.arrived, axis=1)
+        return self.kept.astype(f32) + arrived.astype(f32)
 
 
 def segments(lengths, row_count):
@@ -626,7 +711,7 @@
             place, x_own, x_other, state_in, wsp, wzx, wq, wmix, watt, gain1, seq_col, seq_row, masks, cosine, sine, taps,
             conv_state, bias, rate, skip,
         ),
-        1,
+        1, (), 10 * COST_US,
     )
     own, other = both_parts(part, tensor_count)
     wgu = lax.optimization_barrier((gate_up, part))[0].reshape(model, -1)
@@ -645,14 +730,16 @@
 
     bit = (index % 2).astype(jnp.int32).reshape(1)
     block = model // dp_count
-    cut = ff2 // 4
-
-    def reduction(pairs, after=()):
-        sent, kept = weight_halves(pairs, bit, block, after)
+    cut = max(LANES, ff2 * 3 // 8 // LANES * LANES)
+
+    def reduction(pairs, most, after=()):
+        sent, kept = weight_halves(pairs, bit, block, most, after)
         return Reduction(sent, kept, index, dp_count, block)
 
-    ffn_a = reduction([(dout_rows, hidden, 0, ff2 // 2), (n2, dgu, 0, cut)])
-    order = ffn_a.step()
+    ffn_a = reduction([(dout_rows, hidden, 0, cut)], 768)
+    ffn_b = reduction([(dout_rows, hidden, cut, ff2 // 2), (n2, dgu, 0, ff2)], 768, (ffn_a.kept,))
+    order = ffn_a.step((ffn_b.kept,))
+    order = ffn_b.step(order)
 
     dh1_share, ffn_send, dmix, dy, da, gn2 = call(
         functools.partial(attend_back_kernel, dims, share),
@@ -664,13 +751,13 @@
         (
             place, dn2_own, dn2_other, ffn_part, h1, dout_rows, gain2, wmix, watt, seq_col, seq_row, cosine, sine, pa, y,
         ),
-        1, order,
+        1, order, 40 * COST_US,
     )
     order = ffn_a.step((dmix,))
-    ffn_b = reduction([(n2, dgu, cut, ff2)], order)
-    mix_a = reduction([(dmix, cat, 0, wp + qwp), (act, da, 0, wp + qwp + LANES)], (ffn_b.kept,))
+    mix_out = reduction([(dmix, cat, 0, wp + qwp)], 2048, order)
+    mix_a = reduction([(act, da, 0, wp + qwp + LANES)], 2048, (mix_out.kept,))
     order = ffn_b.step((mix_a.kept,))
-    order = mix_a.step(order)
+    order = mix_out.step(order)
 
     dxb, dact, gn1, gcx, gcs, gstep, gskip = call(
         functools.partial(mixer_back_kernel, dims),
@@ -684,7 +771,7 @@
         (
             pb, dy, y, wzx, state_in, wsp, da, wq, x_rows, seq_col, seq_row, masks, taps, conv_state, bias, rate, skip,
         ),
-        0, order,
+        0, order, 40 * COST_US,
     )
     shared = jnp.concatenate([gn1[0], gn2[0] * (1.0 / tensor_count), gcs.reshape(-1)]).reshape(-1, LANES)
     local = jnp.concatenate([gcx.reshape(-1), gskip.reshape(-1), gstep.reshape(-1)]).reshape(-1, LANES)
@@ -695,11 +782,12 @@
         arrived = exchange(values, dp_count, bit)
         return call(add_kernel, [(values.shape, f32)], [], (values, arrived), 0, after)[0]
 
-    order = ffn_a.step((dxb,))
-    mix_b = reduction([(act, dxb, 0, wp + 384)], order)
-    order = ffn_b.step((mix_b.kept,))
+    order = mix_out.step((dxb,))
+    order = mix_a.step(order)
+    mix_b = reduction([(act, dxb, 0, wp + 384)], 2048, order)
+    order = mix_b.step((mix_b.kept,))
     minor_bit = 1
-    for r in [mix_b, mix_a, ffn_b, mix_b, mix_a] + 4 * [ffn_a, ffn_b, mix_a, mix_b]:
+    for r in [ffn_a, ffn_b, mix_a, mix_out, mix_b, mix_a] + 4 * [ffn_a, ffn_b, mix_out, mix_a, mix_b]:
         if r.done():
             continue
         if minor_bit < dp_count:
@@ -711,15 +799,15 @@
         minor = minor_step(minor, minor_bit, order)
         minor_bit *= 2
     ffn_a, ffn_b, mix_a, mix_b = ffn_a.total(), ffn_b.total(), mix_a.total(), mix_b.total()
-    down_total = ffn_a[:, : ff2 // 2]
-    up_total = jnp.concatenate([ffn_a[:, ff2 // 2 :], ffn_b], axis=1)
-    out_total, first_total = mix_a[:, : wp + qwp], mix_a[:, wp + qwp :]
+    out_total, first_total = mix_out.total(), mix_a
+    down_total = jnp.concatenate([ffn_a, ffn_b[:, : ff2 // 2 - cut]], axis=1)
+    up_total = ffn_b[:, ff2 // 2 - cut :]
     second_total, state_total = mix_b[:, :wp], mix_b[:, wp : wp + 256]
     step_total = mix_b[:, wp + 256 :]
 
     if tensor_count == 2:
         ffn_mine = lax.dynamic_slice_in_dim(ffn_part, me * share, share, 0).astype(f32)
-        ffn_share = ffn_mine + swap(ffn_send).astype(f32)
+        ffn_share = ffn_mine + lax.optimization_barrier((swap(ffn_send), dxb))[0].astype(f32)
     else:
         ffn_share = scatter_rows(ffn_part, me, tensor_count)
     h1_share = lax.dynamic_slice_in_dim(h1, me * share, share, 0)

time: 248 us -> 244 us (0.984)
  waiting for transfers between devices: 75.8 us -> 61.1 us
  starting transfers between devices: 29.2 us -> 38.1 us
  local copies, waits for them, and re-layouts: 24.5 us -> 28.6 us
  Pallas kernels: 96.4 us -> 92.6 us
    pallas_call x24 -> x8, Pallas kernels: 96.4 us -> 52.4 us  [call(): pl.pallas_call(wrapped, out_shape=[jax.ShapeDtypeStruct(s, t) for s, t in...]
    pallas_call x0 -> x20, Pallas kernels: none -> 40.1 us  [the longest x5 20.3 us: weight_halves(): pl.pallas_call(wrapped, out_shape=[jax.ShapeDtypeStruct(s, bf16) for s in...]
    ppermute x20 -> x26, waiting for transfers between devices: 43.8 us -> 30.4 us  [exchange(): return lax.ppermute(sent, 'dp', partners(count, bit))]
    ppermute x20 -> x26, starting transfers between devices: 21.2 us -> 26 us  [exchange(): return lax.ppermute(sent, 'dp', partners(count, bit))]
    unnamed x116 -> x114, local copies, waits for them, and re-layouts: 15.1 us -> 19.6 us
    ppermute x8, starting transfers between devices: 7.98 us -> 12.1 us  [swap(): return lax.ppermute(values, 'tensor', [(0, 1), (1, 0)])]
  transfers between devices with their start and end apart: 28 -> 34, of which waited for: 16 -> 12; matrix products, arithmetic and copies ran while one was open for 14% -> 15% of each run, Pallas kernels for 27% -> 31%
where the time goes in v1:
time: 244 us; the launch traced here: 241 us
  Pallas kernels  92.6 us (38%)
  waiting for transfers between devices  61.1 us (25%)
  starting transfers between devices  38.1 us (16%)
  local copies, waits for them, and re-layouts  28.6 us (12%)
  other arithmetic  16.1 us (7%)
    pallas_call x8, Pallas kernels, call(): pl.pallas_call(wrapped, out_shape=[jax.ShapeDtypeStruct(s, t) for s, t in...  52.4 us
    ppermute x8, waiting for transfers between devices, swap(): return lax.ppermute(values, 'tensor', [(0, 1), (1, 0)])  30.7 us
    ppermute x26, waiting for transfers between devices, exchange(): return lax.ppermute(sent, 'dp', partners(count, bit))  30.4 us
    ppermute x26, starting transfers between devices, exchange(): return lax.ppermute(sent, 'dp', partners(count, bit))  26 us
    pallas_call x5, Pallas kernels, weight_halves(): pl.pallas_call(wrapped, out_shape=[jax.ShapeDtypeStruct(s, bf16) for s in...  20.3 us
    pallas_call x15, Pallas kernels, step_call(): pl.pallas_call(wrapped, out_shape=[jax.ShapeDtypeStruct(half, bf16)] * 2,...  19.9 us
    unnamed x114, local copies, waits for them, and re-layouts  19.6 us
    ppermute x8, starting transfers between devices, swap(): return lax.ppermute(values, 'tensor', [(0, 1), (1, 0)])  12.1 us
  transfers between devices with their start and end apart: 34, of which 12 were waited for; matrix products, arithmetic and copies ran while one was open for 15% of the time, Pallas kernels for 31%

profile of v1, /device:TPU:0, one launch (start us, length us, event | category | flops | bytes accessed | tf_op | source)
XLA Modules:
  0.0 240.7 jit_solution(17848888402677633039)
XLA Ops:
  0.7 3.0 %collective-permute-start = (bf16[192,1024]{1,0:T(8,128)(2,1)}, bf16[192,1024]{1,0:T(8,128)(2,1)S(1)}, u32[]{:S(2)}, u32[]{:S(2)}) collective-permute-start(bf16[192,1024]{1,0:T(8,128)(2,1)} %refs_1_.1), channel_id=1, source_target_pairs={{0,1},{1,0},{2,3},{3,2},{4,5},{5,4},{6,7},{7,6},{8,9},{9,8},{10,11... | collective-permute-start | bytes 1179656 | tf_op jit(solution)/shard_map/ppermute | solution.py:586
  9.0 4.2 %copy.57 = bf16[128,8,2,768]{3,1,2,0:T(8,128)(2,1)} copy(bf16[128,8,2,768]{3,2,1,0:T(2,128)(2,1)} %bitcast.50) | data formatting | bytes 6291456
  15.2 16.6 %shard_map.322 = (bf16[384,1024]{1,0:T(8,128)(2,1)}, bf16[384,1024]{1,0:T(8,128)(2,1)}, f32[384,1152]{1,0:T(8,128)}, f32[384,1152]{1,0:T(8,128)}, f32[384,768]{1...) custom-call(s32[2]{0:T(128)S(1)} %pad_add_fusion.refs_0_, bf16[192,1024]{1,0:T(8,128)(2,1)S(1)} %copy-done.8, ...), custom_call_target="tpu_custom_call" | custom-call | flops 11000000512 | bytes 1000 | tf_op jit(solution)/shard_map/pallas_call | solution.py:575
  31.8 2.0 collective-permute-start.1
  33.9 3.4 %copy.58 = bf16[128,8,2,1024]{3,1,2,0:T(8,128)(2,1)} copy(bf16[128,8,2,1024]{3,2,1,0:T(2,128)(2,1)S(1)} %bitcast.49) | data formatting | bytes 8388608
  38.9 2.2 fusion.18.refs_6_
  41.0 10.0 %collective-permute-done.1.refs_2_ = bf16[384,1024]{1,0:T(8,128)(2,1)S(1)} collective-permute-done((bf16[384,1024]{1,0:T(8,128)(2,1)}, bf16[384,1024]{1,0:T(8,128)(2,1)S(1)}, u32[]{:S(2)}, u32[]{:S(2)}) %collective-permute-start.1) | collective-permute-done | bytes 786464 | tf_op jit(solution)/shard_map/ppermute | solution.py:586
  52.0 8.9 %shard_map.323 = (f32[384,1024]{1,0:T(8,128)}, bf16[384,1024]{1,0:T(8,128)(2,1)S(1)}, bf16[384,1024]{1,0:T(8,128)(2,1)S(1)}, bf16[384,2048]{1,0:T(8,128)(2,1)}, ...) custom-call(bf16[384,1024]{1,0:T(8,128)(2,1)} %get-tuple-element.89.refs_0_.refs_8_, ...), custom_call_target="tpu_custom_call" | custom-call | flops 1000 | bytes 1000 | tf_op jit(solution)/shard_map/pallas_call | solution.py:575
  62.7 3.4 %shard_map.324 = (bf16[512,768]{1,0:T(8,128)(2,1)}, bf16[512,768]{1,0:T(8,128)(2,1)S(1)}) custom-call(s32[1]{0:T(128)} %bitcast.11.bit_ref, bf16[384,1024]{1,0:T(8,128)(2,1)} %copy-done.38, bf16[384,1024]{1,0:T(8,128)(2,1)} %copy-done.2), custom_call_target="tpu_custom_call" | custom-call | flops 1000 | bytes 1000 | tf_op jit(solution)/shard_map/pallas_call | solution.py:428
  67.0 5.9 %shard_map.325 = (bf16[512,768]{1,0:T(8,128)(2,1)}, bf16[512,768]{1,0:T(8,128)(2,1)}, bf16[512,768]{1,0:T(8,128)(2,1)}, bf16[512,2304]{1,0:T(8,128)(2,1)}) custom-call(s32[1]{0:T(128)} %bitcast.11.bit_ref, bf16[384,1024]{1,0:T(8,128)(2,1)} %copy-done.38, bf16[384,1024]{1,0:T(8,128)(2,1)} %copy-done.2, bf16[384,1024]{1,0:T(8,128)(2,1)} %copy-done.10, ...), custom_call_target="tpu_custom_call" | custom-call | flops 1000 | bytes 1000 | tf_op jit(solution)/shard_map/pallas_call | solution.py:428
  78.8 3.0 %shard_map.327 = (bf16[256,2304]{1,0:T(8,128)(2,1)}, bf16[256,2304]{1,0:T(8,128)(2,1)}) custom-call(s32[1]{0:T(128)} %bitcast.10.which_ref, bf16[512,2304]{1,0:T(8,128)(2,1)} %get-tuple-element.102.refs_2_.refs_0_, bf16[512,768]{1,0:T(8,128)(2,1)S(1)} %collective-permute-done.4.refs_1_, bf16[512,768]{1,0:T(8,128)(2,1)S(1)} %collective-permute-done.5.refs_2_, ...), custom_call_target="tpu_custom_call" | custom-call | flops 1000 | bytes 1000 | tf_op jit(solution)/shard_map/pallas_call | solution.py:488
  82.8 11.1 %collective-permute-done.3.refs_2_ = bf16[384,1024]{1,0:T(8,128)(2,1)} collective-permute-done((bf16[384,1024]{1,0:T(8,128)(2,1)}, bf16[384,1024]{1,0:T(8,128)(2,1)}, u32[]{:S(2)}, u32[]{:S(2)}) %collective-permute-start.3) | collective-permute-done | bytes 786464 | tf_op jit(solution)/shard_map/ppermute | solution.py:586
  93.9 12.9 %shard_map.328 = (f32[192,1024]{1,0:T(8,128)}, bf16[192,1024]{1,0:T(8,128)(2,1)S(1)}, bf16[384,1024]{1,0:T(8,128)(2,1)}, f32[384,768]{1,0:T(8,128)}, bf16[384,1152]{1,0:T(8,128)(2,1)}, /*index=5*/f32[1,1024]{1,0:T(1,128)S(1)}) custom-call(s32[2]{0:T(128)S(1)} %copy-done.37, bf16[384,1024]{1,0:T(8,128)(2,1)} %get-tuple-element.95.refs_1_, ...), custom_call_target="tpu_custom_call" | custom-call | flops 44000002048 | bytes 1000 | tf_op jit(solution)/shard_map/pallas_call | solution.py:575
  109.2 3.1 %shard_map.330 = (bf16[512,1024]{1,0:T(8,128)(2,1)}, bf16[512,1024]{1,0:T(8,128)(2,1)}) custom-call(s32[1]{0:T(128)} %bitcast.11.bit_ref, bf16[384,1024]{1,0:T(8,128)(2,1)S(1)} %copy-done.7, bf16[384,1024]{1,0:T(8,128)(2,1)S(1)} %copy-done.11, bf16[128,768]{1,0:T(8,128)(2,1)} %get-tuple-element.116.refs_2_), custom_call_target="tpu_custom_call" | custom-call | flops 1000 | bytes 1000 | tf_op jit(solution)/shard_map/pallas_call | solution.py:428
  112.4 3.5 %shard_map.331 = (bf16[512,1152]{1,0:T(8,128)(2,1)}, bf16[512,1152]{1,0:T(8,128)(2,1)}) custom-call(s32[1]{0:T(128)} %bitcast.11.bit_ref, bf16[384,1024]{1,0:T(8,128)(2,1)S(1)} %copy-done.3, bf16[384,1152]{1,0:T(8,128)(2,1)S(1)} %copy-done.9, bf16[512,1024]{1,0:T(8,128)(2,1)} %get-tuple-element.117.refs_2_.refs_0_), custom_call_target="tpu_custom_call" | custom-call | flops 1000 | bytes 1000 | tf_op jit(solution)/shard_map/pallas_call | solution.py:428
  117.4 2.6 %shard_map.332 = (bf16[128,2304]{1,0:T(8,128)(2,1)}, bf16[128,2304]{1,0:T(8,128)(2,1)S(1)}) custom-call(s32[1]{0:T(128)} %bitcast.12.which_ref, bf16[256,2304]{1,0:T(8,128)(2,1)} %get-tuple-element.119.refs_0_, bf16[256,2304]{1,0:T(8,128)(2,1)} %copy-done.44, bf16[512,1152]{1,0:T(8,128)(2,1)} %get-tuple-element.121.refs_2_.refs_0_), custom_call_target="tpu_custom_call" | custom-call | flops 1000 | bytes 1000 | tf_op jit(solution)/shard_map/pallas_call | solution.py:488
  124.6 14.0 %shard_map.334 = (bf16[384,1152]{1,0:T(8,128)(2,1)}, bf16[384,1024]{1,0:T(8,128)(2,1)}, f32[1,1024]{1,0:T(1,128)S(1)}, f32[4,768]{1,0:T(4,128)S(1)}, f32[4,256]{...) custom-call(f32[384,1152]{1,0:T(8,128)} %get-tuple-element.110.refs_0_, ...), custom_call_target="tpu_custom_call" | custom-call | flops 44000002048 | bytes 1000 | tf_op jit(solution)/shard_map/pallas_call | solution.py:575
  140.1 1.9 shard_map.336
  142.0 4.3 %shard_map.337 = (bf16[512,1152]{1,0:T(8,128)(2,1)}, bf16[512,1152]{1,0:T(8,128)(2,1)}) custom-call(s32[1]{0:T(128)} %bitcast.11.bit_ref, bf16[384,1024]{1,0:T(8,128)(2,1)S(1)} %copy-done.3, bf16[384,1152]{1,0:T(8,128)(2,1)} %get-tuple-element.124.refs_2_.refs_1_, bf16[256,1152]{1,0:T(8,128)(2,1)S(1)} %get-tuple-element.137.refs_2_), custom_call_target="tpu_custom_call" | custom-call | flops 1000 | bytes 1000 | tf_op jit(solution)/shard_map/pallas_call | solution.py:428
  152.1 7.1 %collective-permute-done.8 = bf16[192,1024]{1,0:T(8,128)(2,1)} collective-permute-done((bf16[192,1024]{1,0:T(8,128)(2,1)S(1)}, bf16[192,1024]{1,0:T(8,128)(2,1)}, u32[]{:S(2)}, u32[]{:S(2)}) %collective-permute-start.8) | collective-permute-done | bytes 393248 | tf_op jit(solution)/shard_map/ppermute | solution.py:586
  159.3 2.2 multiply_convert_fusion
  162.2 1.9 shard_map.338
  170.3 7.6 %collective-permute-done.17.refs_1_ = f32[56,128]{1,0:T(8,128)S(1)} collective-permute-done((f32[56,128]{1,0:T(8,128)S(1)}, f32[56,128]{1,0:T(8,128)S(1)}, u32[]{:S(2)}, u32[]{:S(2)}) %collective-permute-start.17) | collective-permute-done | bytes 28704 | tf_op jit(solution)/shard_map/ppermute | solution.py:616
  179.5 2.0 shard_map.342
  181.9 2.7 %collective-permute-start.21 = (f32[56,128]{1,0:T(8,128)S(1)}, f32[56,128]{1,0:T(8,128)S(1)}, u32[]{:S(2)}, u32[]{:S(2)}) collective-permute-start(f32[56,128]{1,0:T(8,128)S(1)} %shard_map.343.refs_2_.refs_0_), channel_id=1, source_target_pairs={{0,16},{2,18},{4,20},{6,22},{8,24},{10,26},{12,28},{14,30},{16,0},... | collective-permute-start | bytes 86024 | tf_op jit(solution)/shard_map/ppermute | solution.py:616
  184.5 2.1 fusion.4
  189.2 2.6 %collective-permute-start.32 = (bf16[64,2304]{1,0:T(8,128)(2,1)}, bf16[64,2304]{1,0:T(8,128)(2,1)}, u32[]{:S(2)}, u32[]{:S(2)}) collective-permute-start(bf16[64,2304]{1,0:T(8,128)(2,1)} %get-tuple-element.144.refs_2_), channel_id=1, source_target_pairs={{0,16},{2,18},{4,20},{6,22},{8,24},{10,26},{12,28},{14,30},{16,0},... | collective-permute-start | bytes 884744 | tf_op jit(solution)/shard_map/ppermute | solution.py:616
  195.0 2.3 collective-permute-done.26.refs_1_
  198.4 2.6 %collective-permute-start.31 = (bf16[64,1024]{1,0:T(8,128)(2,1)S(1)}, bf16[64,1024]{1,0:T(8,128)(2,1)S(1)}, u32[]{:S(2)}, u32[]{:S(2)}) collective-permute-start(bf16[64,1024]{1,0:T(8,128)(2,1)S(1)} %get-tuple-element.150.refs_2_), channel_id=1, source_target_pairs={{0,16},{2,18},{4,20},{6,22},{8,24},{10,26},{12,28},{14,30},{16,0},... | collective-permute-start | bytes 393224 | tf_op jit(solution)/shard_map/ppermute | solution.py:616
  204.5 8.0 %collective-permute-done.31 = bf16[64,1024]{1,0:T(8,128)(2,1)S(1)} collective-permute-done((bf16[64,1024]{1,0:T(8,128)(2,1)S(1)}, bf16[64,1024]{1,0:T(8,128)(2,1)S(1)}, u32[]{:S(2)}, u32[]{:S(2)}) %collective-permute-start.31) | collective-permute-done | bytes 131104 | tf_op jit(solution)/shard_map/ppermute | solution.py:616
  222.4 4.2 %collective-permute-done.28.refs_1_ = bf16[128,1152]{1,0:T(8,128)(2,1)S(1)} collective-permute-done((bf16[128,1152]{1,0:T(8,128)(2,1)S(1)}, bf16[128,1152]{1,0:T(8,128)(2,1)S(1)}, u32[]{:S(2)}, u32[]{:S(2)}) %collective-permute-start.28) | collective-permute-done | bytes 294944 | tf_op jit(solution)/shard_map/ppermute | solution.py:616
  227.9 6.7 %collective-permute-done.29 = bf16[64,1152]{1,0:T(8,128)(2,1)S(1)} collective-permute-done((bf16[64,1152]{1,0:T(8,128)(2,1)S(1)}, bf16[64,1152]{1,0:T(8,128)(2,1)S(1)}, u32[]{:S(2)}, u32[]{:S(2)}) %collective-permute-start.29) | collective-permute-done | bytes 147488 | tf_op jit(solution)/shard_map/ppermute | solution.py:616
  (249 shorter events, 70.6 us)
Async XLA Ops:
  0.7 14.4 %collective-permute-start = (bf16[192,1024]{1,0:T(8,128)(2,1)}, bf16[192,1024]{1,0:T(8,128)(2,1)S(1)}, u32[]{:S(2)}, u32[]{:S(2)}) collective-permute-start(bf16[192,1024]{1,0:T(8,128)(2,1)} %refs_1_.1), channel_id=1, source_target_pairs={{0,1},{1,0},{2,3},{3,2},{4,5},{5,4},{6,7},{7,6},{8,9},{9,8},{10,11... | collective-permute-start | bytes 1179656 | tf_op jit(solution)/shard_map/ppermute | solution.py:586
  15.1 22.2 %collective-permute-start.2 = (bf16[192,1024]{1,0:T(8,128)(2,1)S(1)}, bf16[192,1024]{1,0:T(8,128)(2,1)S(1)}, u32[]{:S(2)}, u32[]{:S(2)}) collective-permute-start(bf16[192,1024]{1,0:T(8,128)(2,1)S(1)} %copy-done.49), channel_id=1, source_target_pairs={{0,1},{1,0},{2,3},{3,2},{4,5},{5,4},{6,7},{7,6},{8,9},{9,8},{10,11... | collective-permute-start | bytes 1179656 | tf_op jit(solution)/shard_map/ppermute | solution.py:586
  31.8 19.3 %collective-permute-start.1 = (bf16[384,1024]{1,0:T(8,128)(2,1)}, bf16[384,1024]{1,0:T(8,128)(2,1)S(1)}, u32[]{:S(2)}, u32[]{:S(2)}) collective-permute-start(bf16[384,1024]{1,0:T(8,128)(2,1)} %get-tuple-element.90.refs_1_), channel_id=1, source_target_pairs={{0,1},{1,0},{2,3},{3,2},{4,5},{5,4},{6,7},{7,6},{8,9},{9,8},{10,11... | collective-permute-start | bytes 2359304 | tf_op jit(solution)/shard_map/ppermute | solution.py:586
  67.0 8.7 %collective-permute-start.7 = (bf16[512,768]{1,0:T(8,128)(2,1)}, bf16[512,768]{1,0:T(8,128)(2,1)}, u32[]{:S(2)}, u32[]{:S(2)}) collective-permute-start(bf16[512,768]{1,0:T(8,128)(2,1)} %get-tuple-element.106), channel_id=1, source_target_pairs={{0,2},{2,0},{4,6},{6,4},{8,10},{10,8},{12,14},{14,12},{16,18},{18,... | collective-permute-start | bytes 2359304 | tf_op jit(solution)/shard_map/ppermute | solution.py:616
  73.0 5.8 %collective-permute-start.4 = (bf16[512,768]{1,0:T(8,128)(2,1)}, bf16[512,768]{1,0:T(8,128)(2,1)S(1)}, u32[]{:S(2)}, u32[]{:S(2)}) collective-permute-start(bf16[512,768]{1,0:T(8,128)(2,1)} %get-tuple-element.103), channel_id=1, source_target_pairs={{0,2},{2,0},{4,6},{6,4},{8,10},{10,8},{12,14},{14,12},{16,18},{18,... | collective-permute-start | bytes 2359304 | tf_op jit(solution)/shard_map/ppermute | solution.py:616
  73.6 5.2 %collective-permute-start.5 = (bf16[512,768]{1,0:T(8,128)(2,1)}, bf16[512,768]{1,0:T(8,128)(2,1)S(1)}, u32[]{:S(2)}, u32[]{:S(2)}) collective-permute-start(bf16[512,768]{1,0:T(8,128)(2,1)} %get-tuple-element.104), channel_id=1, source_target_pairs={{0,2},{2,0},{4,6},{6,4},{8,10},{10,8},{12,14},{14,12},{16,18},{18,... | collective-permute-start | bytes 2359304 | tf_op jit(solution)/shard_map/ppermute | solution.py:616
  73.6 5.1 %collective-permute-start.6 = (bf16[512,768]{1,0:T(8,128)(2,1)}, bf16[512,768]{1,0:T(8,128)(2,1)}, u32[]{:S(2)}, u32[]{:S(2)}) collective-permute-start(bf16[512,768]{1,0:T(8,128)(2,1)} %get-tuple-element.105), channel_id=1, source_target_pairs={{0,2},{2,0},{4,6},{6,4},{8,10},{10,8},{12,14},{14,12},{16,18},{18,... | collective-permute-start | bytes 2359304 | tf_op jit(solution)/shard_map/ppermute | solution.py:616
  74.1 19.8 %collective-permute-start.3 = (bf16[384,1024]{1,0:T(8,128)(2,1)}, bf16[384,1024]{1,0:T(8,128)(2,1)}, u32[]{:S(2)}, u32[]{:S(2)}) collective-permute-start(bf16[384,1024]{1,0:T(8,128)(2,1)} %get-tuple-element.95.refs_1_), channel_id=1, source_target_pairs={{0,1},{1,0},{2,3},{3,2},{4,5},{5,4},{6,7},{7,6},{8,9},{9,8},{10,11... | collective-permute-start | bytes 2359304 | tf_op jit(solution)/shard_map/ppermute | solution.py:586
  77.2 29.6 %collective-permute-start.9 = (bf16[256,768]{1,0:T(8,128)(2,1)S(1)}, bf16[256,768]{1,0:T(8,128)(2,1)S(1)}, u32[]{:S(2)}, u32[]{:S(2)}) collective-permute-start(bf16[256,768]{1,0:T(8,128)(2,1)S(1)} %get-tuple-element.107.refs_4_), channel_id=1, source_target_pairs={{0,4},{2,6},{4,0},{6,2},{8,12},{10,14},{12,8},{14,10},{16,20},{18,... | collective-permute-start | bytes 1179656 | tf_op jit(solution)/shard_map/ppermute | solution.py:616
  81.8 34.6 %collective-permute-start.11 = (bf16[256,2304]{1,0:T(8,128)(2,1)}, bf16[256,2304]{1,0:T(8,128)(2,1)S(1)}, u32[]{:S(2)}, u32[]{:S(2)}) collective-permute-start(bf16[256,2304]{1,0:T(8,128)(2,1)} %get-tuple-element.108.refs_15_), channel_id=1, source_target_pairs={{0,4},{2,6},{4,0},{6,2},{8,12},{10,14},{12,8},{14,10},{16,20},{18,... | collective-permute-start | bytes 3538952 | tf_op jit(solution)/shard_map/ppermute | solution.py:616
  112.3 7.8 %collective-permute-start.10 = (bf16[512,1024]{1,0:T(8,128)(2,1)}, bf16[512,1024]{1,0:T(8,128)(2,1)S(1)}, u32[]{:S(2)}, u32[]{:S(2)}) collective-permute-start(bf16[512,1024]{1,0:T(8,128)(2,1)} %get-tuple-element.118), channel_id=1, source_target_pairs={{0,2},{2,0},{4,6},{6,4},{8,10},{10,8},{12,14},{14,12},{16,18},{18,... | collective-permute-start | bytes 3145736 | tf_op jit(solution)/shard_map/ppermute | solution.py:616
  115.9 23.2 %collective-permute-start.14 = (bf16[512,1152]{1,0:T(8,128)(2,1)}, bf16[512,1152]{1,0:T(8,128)(2,1)S(1)}, u32[]{:S(2)}, u32[]{:S(2)}) collective-permute-start(bf16[512,1152]{1,0:T(8,128)(2,1)} %get-tuple-element.134), channel_id=1, source_target_pairs={{0,2},{2,0},{4,6},{6,4},{8,10},{10,8},{12,14},{14,12},{16,18},{18,... | collective-permute-start | bytes 3538952 | tf_op jit(solution)/shard_map/ppermute | solution.py:616
  122.8 15.8 %collective-permute-start.15 = (bf16[256,1024]{1,0:T(8,128)(2,1)S(1)}, bf16[256,1024]{1,0:T(8,128)(2,1)S(1)}, u32[]{:S(2)}, u32[]{:S(2)}) collective-permute-start(bf16[256,1024]{1,0:T(8,128)(2,1)S(1)} %get-tuple-element.123.refs_17_), channel_id=1, source_target_pairs={{0,4},{2,6},{4,0},{6,2},{8,12},{10,14},{12,8},{14,10},{16,20},{18,... | collective-permute-start | bytes 1572872 | tf_op jit(solution)/shard_map/ppermute | solution.py:616
  146.4 15.1 %collective-permute-start.16 = (bf16[512,1152]{1,0:T(8,128)(2,1)}, bf16[512,1152]{1,0:T(8,128)(2,1)}, u32[]{:S(2)}, u32[]{:S(2)}) collective-permute-start(bf16[512,1152]{1,0:T(8,128)(2,1)} %get-tuple-element.139), channel_id=1, source_target_pairs={{0,2},{2,0},{4,6},{6,4},{8,10},{10,8},{12,14},{14,12},{16,18},{18,... | collective-permute-start | bytes 3538952 | tf_op jit(solution)/shard_map/ppermute | solution.py:616
  147.2 12.0 %collective-permute-start.8 = (bf16[192,1024]{1,0:T(8,128)(2,1)S(1)}, bf16[192,1024]{1,0:T(8,128)(2,1)}, u32[]{:S(2)}, u32[]{:S(2)}) collective-permute-start(bf16[192,1024]{1,0:T(8,128)(2,1)S(1)} %get-tuple-element.109), channel_id=1, source_target_pairs={{0,1},{1,0},{2,3},{3,2},{4,5},{5,4},{6,7},{7,6},{8,9},{9,8},{10,11... | collective-permute-start | bytes 1179656 | tf_op jit(solution)/shard_map/ppermute | solution.py:586
  148.8 19.8 %collective-permute-start.18 = (bf16[128,768]{1,0:T(8,128)(2,1)}, bf16[128,768]{1,0:T(8,128)(2,1)}, u32[]{:S(2)}, u32[]{:S(2)}) collective-permute-start(bf16[128,768]{1,0:T(8,128)(2,1)} %get-tuple-element.116.refs_2_), channel_id=1, source_target_pairs={{0,8},{2,10},{4,12},{6,14},{8,0},{10,2},{12,4},{14,6},{16,24},{18,... | collective-permute-start | bytes 589832 | tf_op jit(solution)/shard_map/ppermute | solution.py:616
  150.4 29.2 %collective-permute-start.20 = (bf16[128,2304]{1,0:T(8,128)(2,1)}, bf16[128,2304]{1,0:T(8,128)(2,1)}, u32[]{:S(2)}, u32[]{:S(2)}) collective-permute-start(bf16[128,2304]{1,0:T(8,128)(2,1)} %get-tuple-element.122.refs_2_), channel_id=1, source_target_pairs={{0,8},{2,10},{4,12},{6,14},{8,0},{10,2},{12,4},{14,6},{16,24},{18,... | collective-permute-start | bytes 1769480 | tf_op jit(solution)/shard_map/ppermute | solution.py:616
  151.6 15.7 %collective-permute-start.12 = (bf16[192,1024]{1,0:T(8,128)(2,1)}, bf16[192,1024]{1,0:T(8,128)(2,1)}, u32[]{:S(2)}, u32[]{:S(2)}) collective-permute-start(bf16[192,1024]{1,0:T(8,128)(2,1)} %dynamic-slice_bitcast_fusion), channel_id=1, source_target_pairs={{0,1},{1,0},{2,3},{3,2},{4,5},{5,4},{6,7},{7,6},{8,9},{9,8},{10,11... | collective-permute-start | bytes 1179656 | tf_op jit(solution)/shard_map/ppermute | solution.py:586
  159.3 4.9 %collective-permute-start.13 = (f32[56,128]{1,0:T(8,128)S(1)}, f32[56,128]{1,0:T(8,128)S(1)}, u32[]{:S(2)}, u32[]{:S(2)}) collective-permute-start(f32[56,128]{1,0:T(8,128)S(1)} %pad_maximum_fusion.3.refs_0_), channel_id=1, source_target_pairs={{0,2},{2,0},{4,6},{6,4},{8,10},{10,8},{12,14},{14,12},{16,18},{18,... | collective-permute-start | bytes 86024 | tf_op jit(solution)/shard_map/ppermute | solution.py:616
  161.5 27.7 %collective-permute-start.22 = (bf16[256,1152]{1,0:T(8,128)(2,1)S(1)}, bf16[256,1152]{1,0:T(8,128)(2,1)S(1)}, u32[]{:S(2)}, u32[]{:S(2)}) collective-permute-start(bf16[256,1152]{1,0:T(8,128)(2,1)S(1)} %get-tuple-element.137.refs_2_), channel_id=1, source_target_pairs={{0,4},{2,6},{4,0},{6,2},{8,12},{10,14},{12,8},{14,10},{16,20},{18,... | collective-permute-start | bytes 1769480 | tf_op jit(solution)/shard_map/ppermute | solution.py:616
  164.2 13.6 %collective-permute-start.17 = (f32[56,128]{1,0:T(8,128)S(1)}, f32[56,128]{1,0:T(8,128)S(1)}, u32[]{:S(2)}, u32[]{:S(2)}) collective-permute-start(f32[56,128]{1,0:T(8,128)S(1)} %shard_map.339.refs_2_.refs_0_), channel_id=1, source_target_pairs={{0,4},{2,6},{4,0},{6,2},{8,12},{10,14},{12,8},{14,10},{16,20},{18,... | collective-permute-start | bytes 86024 | tf_op jit(solution)/shard_map/ppermute | solution.py:616
  181.9 11.0 %collective-permute-start.21 = (f32[56,128]{1,0:T(8,128)S(1)}, f32[56,128]{1,0:T(8,128)S(1)}, u32[]{:S(2)}, u32[]{:S(2)}) collective-permute-start(f32[56,128]{1,0:T(8,128)S(1)} %shard_map.343.refs_2_.refs_0_), channel_id=1, source_target_pairs={{0,16},{2,18},{4,20},{6,22},{8,24},{10,26},{12,28},{14,30},{16,0},... | collective-permute-start | bytes 86024 | tf_op jit(solution)/shard_map/ppermute | solution.py:616
  186.6 10.8 %collective-permute-start.26 = (bf16[128,1024]{1,0:T(8,128)(2,1)S(1)}, bf16[128,1024]{1,0:T(8,128)(2,1)S(1)}, u32[]{:S(2)}, u32[]{:S(2)}) collective-permute-start(bf16[128,1024]{1,0:T(8,128)(2,1)S(1)} %copy-done.18), channel_id=1, source_target_pairs={{0,8},{2,10},{4,12},{6,14},{8,0},{10,2},{12,4},{14,6},{16,24},{18,... | collective-permute-start | bytes 786440 | tf_op jit(solution)/shard_map/ppermute | solution.py:616
  188.2 14.7 %collective-permute-start.33 = (bf16[64,768]{1,0:T(8,128)(2,1)}, bf16[64,768]{1,0:T(8,128)(2,1)}, u32[]{:S(2)}, u32[]{:S(2)}) collective-permute-start(bf16[64,768]{1,0:T(8,128)(2,1)} %get-tuple-element.142.refs_2_), channel_id=1, source_target_pairs={{0,16},{2,18},{4,20},{6,22},{8,24},{10,26},{12,28},{14,30},{16,0},... | collective-permute-start | bytes 294920 | tf_op jit(solution)/shard_map/ppermute | solution.py:616
  188.5 25.3 %collective-permute-start.25 = (bf16[256,1152]{1,0:T(8,128)(2,1)S(1)}, bf16[256,1152]{1,0:T(8,128)(2,1)S(1)}, u32[]{:S(2)}, u32[]{:S(2)}) collective-permute-start(bf16[256,1152]{1,0:T(8,128)(2,1)S(1)} %get-tuple-element.140.refs_2_), channel_id=1, source_target_pairs={{0,4},{2,6},{4,0},{6,2},{8,12},{10,14},{12,8},{14,10},{16,20},{18,... | collective-permute-start | bytes 1769480 | tf_op jit(solution)/shard_map/ppermute | solution.py:616
  189.2 26.3 %collective-permute-start.32 = (bf16[64,2304]{1,0:T(8,128)(2,1)}, bf16[64,2304]{1,0:T(8,128)(2,1)}, u32[]{:S(2)}, u32[]{:S(2)}) collective-permute-start(bf16[64,2304]{1,0:T(8,128)(2,1)} %get-tuple-element.144.refs_2_), channel_id=1, source_target_pairs={{0,16},{2,18},{4,20},{6,22},{8,24},{10,26},{12,28},{14,30},{16,0},... | collective-permute-start | bytes 884744 | tf_op jit(solution)/shard_map/ppermute | solution.py:616
  192.9 5.5 %collective-permute-start.23 = (f32[24,128]{1,0:T(8,128)S(1)}, f32[24,128]{1,0:T(8,128)S(1)}, u32[]{:S(2)}, u32[]{:S(2)}) collective-permute-start(f32[24,128]{1,0:T(8,128)S(1)} %slice.109), channel_id=1, source_target_pairs={{0,1},{1,0},{2,3},{3,2},{4,5},{5,4},{6,7},{7,6},{8,9},{9,8},{10,11... | collective-permute-start | bytes 36872 | tf_op jit(solution)/shard_map/ppermute | solution.py:586
  197.3 17.0 %collective-permute-start.24 = (bf16[128,1152]{1,0:T(8,128)(2,1)}, bf16[128,1152]{1,0:T(8,128)(2,1)S(1)}, u32[]{:S(2)}, u32[]{:S(2)}) collective-permute-start(bf16[128,1152]{1,0:T(8,128)(2,1)} %get-tuple-element.146.refs_2_), channel_id=1, source_target_pairs={{0,8},{2,10},{4,12},{6,14},{8,0},{10,2},{12,4},{14,6},{16,24},{18,... | collective-permute-start | bytes 884744 | tf_op jit(solution)/shard_map/ppermute | solution.py:616
  198.4 14.0 %collective-permute-start.31 = (bf16[64,1024]{1,0:T(8,128)(2,1)S(1)}, bf16[64,1024]{1,0:T(8,128)(2,1)S(1)}, u32[]{:S(2)}, u32[]{:S(2)}) collective-permute-start(bf16[64,1024]{1,0:T(8,128)(2,1)S(1)} %get-tuple-element.150.refs_2_), channel_id=1, source_target_pairs={{0,16},{2,18},{4,20},{6,22},{8,24},{10,26},{12,28},{14,30},{16,0},... | collective-permute-start | bytes 393224 | tf_op jit(solution)/shard_map/ppermute | solution.py:616
  214.7 7.1 %collective-permute-start.27 = (bf16[64,1152]{1,0:T(8,128)(2,1)S(1)}, bf16[64,1152]{1,0:T(8,128)(2,1)S(1)}, u32[]{:S(2)}, u32[]{:S(2)}) collective-permute-start(bf16[64,1152]{1,0:T(8,128)(2,1)S(1)} %get-tuple-element.153.refs_2_), channel_id=1, source_target_pairs={{0,16},{2,18},{4,20},{6,22},{8,24},{10,26},{12,28},{14,30},{16,0},... | collective-permute-start | bytes 442376 | tf_op jit(solution)/shard_map/ppermute | solution.py:616
  218.6 8.0 %collective-permute-start.28 = (bf16[128,1152]{1,0:T(8,128)(2,1)S(1)}, bf16[128,1152]{1,0:T(8,128)(2,1)S(1)}, u32[]{:S(2)}, u32[]{:S(2)}) collective-permute-start(bf16[128,1152]{1,0:T(8,128)(2,1)S(1)} %get-tuple-element.151.refs_2_), channel_id=1, source_target_pairs={{0,8},{2,10},{4,12},{6,14},{8,0},{10,2},{12,4},{14,6},{16,24},{18,... | collective-permute-start | bytes 884744 | tf_op jit(solution)/shard_map/ppermute | solution.py:616
  226.9 7.7 %collective-permute-start.29 = (bf16[64,1152]{1,0:T(8,128)(2,1)S(1)}, bf16[64,1152]{1,0:T(8,128)(2,1)S(1)}, u32[]{:S(2)}, u32[]{:S(2)}) collective-permute-start(bf16[64,1152]{1,0:T(8,128)(2,1)S(1)} %get-tuple-element.156), channel_id=1, source_target_pairs={{0,16},{2,18},{4,20},{6,22},{8,24},{10,26},{12,28},{14,30},{16,0},... | collective-permute-start | bytes 442376 | tf_op jit(solution)/shard_map/ppermute | solution.py:616
  (56 other events, 372.7 us)

commit v2 on v1

--- a/solution.py
+++ b/solution.py
@@ -284,9 +284,9 @@
 
 
 def mixer_back_kernel(
-    dims, pb_ref, dy_ref, y_ref, wzx_ref, wbc_ref, wsp_ref, da_ref, wq_ref, x_ref, seqc_ref, seqr_ref, masks_ref,
-    convx_ref, convs_ref, bias_ref, rate_ref, skip_ref,
-    dxb_ref, dact_ref, gn1_ref, gcx_ref, gcs_ref, gstep_ref, gskip_ref,
+    dims, share, place_ref, pb_ref, dy_ref, y_ref, wzx_ref, wbc_ref, wsp_ref, da_ref, wq_ref, x_ref, seqc_ref, seqr_ref, masks_ref,
+    convx_ref, convs_ref, bias_ref, rate_ref, skip_ref, gn2_ref,
+    dxb_ref, dact_ref, dact_send_ref, small_ref,
     neg_ref, gt_ref, dgt_ref, dsum_ref, ddir_ref,
 ):
     heads, qheads, wp, qwp, span = dims
@@ -305,6 +305,7 @@
     bcc = (sconv * ssig).astype(bf16)
     bm, cm = bcc[:, :128], bcc[:, 128:]
     gt_ref[...] = mm_nt(bm, cm)
+    small_ref[...] = jnp.zeros_like(small_ref)
     dgt_ref[...] = jnp.zeros_like(dgt_ref)
     for p in range(wp // LANES):
         cols = slice(p * LANES, (p + 1) * LANES)
@@ -318,7 +319,7 @@
         skip = skip_ref[:, cols]
         scanned = y_ref[:, cols] - skip * xc
         dy = dy_ref[:, cols]
-        gskip_ref[:, cols] = jnp.sum(dy * xc, axis=0, keepdims=True)
+        small_ref[6:7, cols] = jnp.sum(dy * xc, axis=0, keepdims=True)
         dyb = dy.astype(bf16)
         blocks = []
         for a in range(rows // span):
@@ -337,13 +338,13 @@
         dsum_ref[:, cols] = dyb.astype(f32) * scanned - xdt.astype(f32) * dxdt
         ddir_ref[:, cols] = dxdt * xc
         dconv = (dxdt * dt_cols + skip * dy) * (csig * (1.0 + conv * (1.0 - csig)))
-        gcx_ref[:, cols] = jnp.concatenate([jnp.sum(t * dconv, axis=0, keepdims=True) for t in terms], axis=0)
+        small_ref[2:6, cols] = jnp.concatenate([jnp.sum(t * dconv, axis=0, keepdims=True) for t in terms], axis=0)
         dxb_ref[:, cols] = conv_back(dconv, masks, convx_ref[:, cols]).astype(bf16)
 
     dgt = dgt_ref[...].astype(bf16)
     dbcc = jnp.concatenate([mm(dgt, cm), mm_tn(dgt, bm)], axis=1)
     dsconv = dbcc * (ssig * (1.0 + sconv * (1.0 - ssig)))
-    gcs_ref[...] = jnp.concatenate([jnp.sum(t * dsconv, axis=0, keepdims=True) for t in sterms], axis=0)
+    small_ref[2:6, wp : wp + 256] = jnp.concatenate([jnp.sum(t * dsconv, axis=0, keepdims=True) for t in sterms], axis=0)
     dxb_ref[:, wp : wp + 256] = conv_back(dsconv, masks, convs_ref[...]).astype(bf16)
 
     head_of = lax.broadcasted_iota(jnp.int32, (wp, LANES), 0) // HD
@@ -356,18 +357,20 @@
     dstep = ddt * jax.nn.sigmoid(pb_ref[:, wp + 256 :] + bias_ref[...])
     dstep = jnp.where(lane_ids(rows) < heads, dstep, 0.0)
     dxb_ref[:, wp + 256 :] = dstep.astype(bf16)
-    gstep_ref[...] = jnp.concatenate(
-        [jnp.sum(dstep, axis=0, keepdims=True), -rate * jnp.sum(dt * dlog, axis=0, keepdims=True)], axis=0
-    )
+    small_ref[6:7, wp : wp + LANES] = jnp.sum(dstep, axis=0, keepdims=True)
+    small_ref[6:7, wp + LANES : wp + 256] = -rate * jnp.sum(dt * dlog, axis=0, keepdims=True)
     finish(dxb_ref)
     dact = mm_nt(da_ref[:, :wp], wzx_ref[:, :wp]) + mm_nt(dxb_ref[:, :wp], wzx_ref[:, wp:])
     dact = dact + mm_nt(dxb_ref[:, wp : wp + 256], wbc_ref[...]) + mm_nt(da_ref[:, wp : wp + qwp], wq_ref[...])
     dact = dact + mm_nt(dxb_ref[:, wp + 256 :], wsp_ref[:, :LANES]) + mm_nt(da_ref[:, wp + qwp :], wsp_ref[:, LANES:])
     dact_ref[...] = dact.astype(bf16)
     finish(dact_ref)
+    dact_send_ref[...] = dact_ref[pl.ds(pl.multiple_of(place_ref[1] * share, 16), share), :]
+    finish(dact_send_ref)
     x = x_ref[...].astype(f32)
     r1 = lax.rsqrt(jnp.mean(x * x, axis=-1, keepdims=True) + norm_eps)
-    gn1_ref[...] = jnp.sum(dact * x * r1, axis=0, keepdims=True)
+    small_ref[0:1, :] = jnp.sum(dact * x * r1, axis=0, keepdims=True)
+    small_ref[1:2, :] = gn2_ref[...] * (share / rows)
 
 
 def pieces_of(width, most):
@@ -380,7 +383,7 @@
 def grad_kernel(cuts, pieces, block, bit_ref, *refs):
     pairs = len(cuts)
     ins, refs = refs[: 2 * pairs], refs[2 * pairs :]
-    sents, kept, refs = refs[: len(pieces)], refs[len(pieces)], refs[len(pieces) + 1 :]
+    sents, kepts, refs = refs[: len(pieces)], refs[len(pieces) : 2 * len(pieces)], refs[2 * len(pieces) :]
     buffers, refs = refs[: 2 * pairs], refs[2 * pairs :]
     turned, stage, in_sems, sent_sems, kept_sems = refs
     fetched = [Fetched(ins[i], buffers[i], in_sems.at[i]) for i in range(2 * pairs)]
@@ -399,7 +402,7 @@
             while sent_to < len(pieces) and pieces[sent_to][1] <= at:
                 cols = pl.ds(pieces[sent_to][0], pieces[sent_to][1] - pieces[sent_to][0])
                 copies.append(pltpu.make_async_copy(stage.at[0, :, cols], sents[sent_to], sent_sems.at[sent_to]))
-                copies.append(pltpu.make_async_copy(stage.at[1, :, cols], kept.at[:, cols], kept_sems.at[sent_to]))
+                copies.append(pltpu.make_async_copy(stage.at[1, :, cols], kepts[sent_to], kept_sems.at[sent_to]))
                 copies[-2].start()
                 copies[-1].start()
                 sent_to += 1
@@ -420,16 +423,16 @@
     rows, model = pairs[0][0].shape
     width = sum(high - low for low, high in cuts)
     pieces = pieces_of(width, most)
-    outs = [(model // 2, high - low) for low, high in pieces] + [(model // 2, width)]
+    outs = [(model // 2, high - low) for low, high in pieces] * 2
 
     def wrapped(bit_ref, *refs):
         grad_kernel(cuts, pieces, block, bit_ref, *refs[: len(args)], *refs[len(args) + len(after) :])
 
-    *sent, kept = pl.pallas_call(
+    outs = pl.pallas_call(
         wrapped,
         out_shape=[jax.ShapeDtypeStruct(s, bf16) for s in outs],
-        in_specs=[pl.BlockSpec(memory_space=pltpu.SMEM)] + [pl.BlockSpec(memory_space=pl.ANY)] * (len(args) + len(after)),
-        out_specs=[pl.BlockSpec(memory_space=pl.ANY)] * len(outs),
+        in_specs=[pl.BlockSpec(memory_space=pltpu.SMEM)] + [pl.BlockSpec(memory_space=pltpu.HBM)] * (len(args) + len(after)),
+        out_specs=[pl.BlockSpec(memory_space=pltpu.HBM)] * len(outs),
         scratch_shapes=[pltpu.VMEM(a.shape, a.dtype) for a in args]
         + [
             pltpu.VMEM((model, rows), bf16), pltpu.VMEM((2, model // 2, width), bf16),
@@ -438,67 +441,69 @@
         ],
         **plain_params(),
     )(bit, *args, *after)
-    return sent, kept
-
-
-def step_kernel(pieces, whole, block, which_ref, kept, *refs):
-    count = 1 if whole else len(pieces)
-    arrived, refs = refs[:count], refs[count:]
-    away, mine, kept_buf, arrived_buf, away_buf, mine_buf, kept_sems, arrived_sems, away_sems, mine_sems = refs
+    return outs[: len(pieces)], outs[len(pieces) :]
+
+
+def step_kernel(pieces, sources, block, small, which_ref, *refs):
+    arrays, refs = refs[: 2 * sources], refs[2 * sources :]
+    if small:
+        small_own, small_other, refs = refs[0], refs[1], refs[2:]
+    away, mine, refs = refs[0], refs[1], refs[2:]
+    if small:
+        small_ref, refs = refs[0], refs[1:]
+    kept_buf, arrived_buf, away_buf, mine_buf, kept_sems, arrived_sems, away_sems, mine_sems = refs
     which = which_ref[0]
     ins, outs = [], []
-    for k, (low, high) in enumerate(pieces):
-        cols = pl.ds(low, high - low)
-        source = arrived[0].at[:, cols] if whole else arrived[k]
-        ins.append(pltpu.make_async_copy(kept.at[:, cols], kept_buf.at[:, cols], kept_sems.at[k]))
-        ins.append(pltpu.make_async_copy(source, arrived_buf.at[:, cols], arrived_sems.at[k]))
+    for k, (source, low, at, width) in enumerate(pieces):
+        cols, here = pl.ds(low, width), pl.ds(at, width)
+        ins.append(pltpu.make_async_copy(arrays[2 * source].at[:, cols], kept_buf.at[:, here], kept_sems.at[k]))
+        ins.append(pltpu.make_async_copy(arrays[2 * source + 1].at[:, cols], arrived_buf.at[:, here], arrived_sems.at[k]))
         ins[-2].start()
         ins[-1].start()
-    for k, (low, high) in enumerate(pieces):
+    if small:
+        small_ref[...] = small_own[...] + small_other[...]
+    for k, (source, low, at, width) in enumerate(pieces):
         ins[2 * k].wait()
         ins[2 * k + 1].wait()
-        cols = pl.ds(low, high - low)
+        here = pl.ds(at, width)
         for out, target, sems, side in ((away_buf, away, away_sems, 1 - which), (mine_buf, mine, mine_sems, which)):
-            for i in range(kept.shape[0] // (2 * block)):
+            for i in range(kept_buf.shape[0] // (2 * block)):
                 rows = pl.ds(pl.multiple_of((2 * i + side) * block, block), block)
-                total = kept_buf[rows, low:high].astype(f32) + arrived_buf[rows, low:high].astype(f32)
-                out[i * block : (i + 1) * block, low:high] = total.astype(bf16)
-            outs.append(pltpu.make_async_copy(out.at[:, cols], target.at[:, cols], sems.at[k]))
+                total = kept_buf[rows, at : at + width].astype(f32) + arrived_buf[rows, at : at + width].astype(f32)
+                out[i * block : (i + 1) * block, at : at + width] = total.astype(bf16)
+            outs.append(pltpu.make_async_copy(out.at[:, here], target.at[:, here], sems.at[k]))
             outs[-1].start()
     for copy in outs:
         copy.wait()
 
 
-def step_call(which, kept, arrived, block, after):
-    rows, width = kept.shape
-    whole = len(arrived) == 1
-    if whole:
-        pieces = pieces_of(width, 512)
-    else:
-        edges = [0]
-        for a in arrived:
-            edges.append(edges[-1] + a.shape[1])
-        pieces = list(zip(edges[:-1], edges[1:]))
-    used = 1 + len(arrived)
+def step_call(which, sources, block, after, small=()):
+    rows = sources[0][0].shape[0]
+    pieces, at = [], 0
+    for i, (kept, _) in enumerate(sources):
+        for low, high in pieces_of(kept.shape[1], 512):
+            pieces.append((i, low, at + low, high - low))
+        at += kept.shape[1]
+    args = [a for pair in sources for a in pair]
 
     def wrapped(which_ref, *refs):
-        step_kernel(pieces, whole, block, which_ref, *refs[:used], *refs[used + len(after) :])
-
-    half = (rows // 2, width)
+        used = len(args) + len(small)
+        step_kernel(pieces, len(sources), block, bool(small), which_ref, *refs[:used], *refs[used + len(after) :])
+
+    half = (rows // 2, at)
+    anywhere = pl.BlockSpec(memory_space=pltpu.HBM)
+    inside = pl.BlockSpec(memory_space=pltpu.VMEM)
     return pl.pallas_call(
         wrapped,
-        out_shape=[jax.ShapeDtypeStruct(half, bf16)] * 2,
-        in_specs=[pl.BlockSpec(memory_space=pltpu.SMEM)] + [pl.BlockSpec(memory_space=pl.ANY)] * (used + len(after)),
-        out_specs=[pl.BlockSpec(memory_space=pl.ANY)] * 2,
-        scratch_shapes=[pltpu.VMEM((rows, width), bf16)] * 2
+        out_shape=[jax.ShapeDtypeStruct(half, bf16)] * 2 + [jax.ShapeDtypeStruct(a.shape, f32) for a in small[:1]],
+        in_specs=[pl.BlockSpec(memory_space=pltpu.SMEM)] + [anywhere] * len(args) + [inside] * len(small)
+        + [anywhere] * len(after),
+        out_specs=[anywhere] * 2 + [inside] * len(small[:1]),
+        scratch_shapes=[pltpu.VMEM((rows, at), bf16)] * 2
         + [pltpu.VMEM(half, bf16)] * 2
         + [pltpu.SemaphoreType.DMA((len(pieces),))] * 4,
         **plain_params(),
-    )(which, kept, *arrived, *after)
-
-
-def add_kernel(a_ref, b_ref, out_ref):
-    out_ref[...] = a_ref[...] + b_ref[...]
+    )(which, *args, *small, *after)
 
 
 class Fetched:
@@ -571,12 +576,12 @@
             if isinstance(ref, Stored):
                 ref.copy.wait()
 
-    spaces = [pltpu.SMEM] * scalars + [pl.ANY if big else pltpu.VMEM for big in large_in[scalars:]] + [pl.ANY] * len(after)
+    spaces = [pltpu.SMEM] * scalars + [pltpu.HBM if big else pltpu.VMEM for big in large_in[scalars:]] + [pltpu.HBM] * len(after)
     return pl.pallas_call(
         wrapped,
         out_shape=[jax.ShapeDtypeStruct(s, t) for s, t in outs],
         in_specs=[pl.BlockSpec(memory_space=space) for space in spaces],
-        out_specs=[pl.BlockSpec(memory_space=pl.ANY if big else pltpu.VMEM) for big in large_out],
+        out_specs=[pl.BlockSpec(memory_space=pltpu.HBM if big else pltpu.VMEM) for big in large_out],
         scratch_shapes=buffers + [pltpu.SemaphoreType.DMA((max(copies, 1),))] + [pltpu.VMEM(s, t) for s, t in scratch],
         **plain_params(flops),
     )(*args, *after)
@@ -617,10 +622,10 @@
 
 
 class Reduction:
-    def __init__(self, sent, kept, index, count, block):
-        self.index, self.count, self.block, self.bit = index, count, block, 1
-        self.kept = kept
-        self.arrived = [exchange(part, count, 1) for part in sent]
+    def __init__(self, parts, index, count, block, bit=1, small=None):
+        self.parts, self.index, self.count, self.block, self.bit = parts, index, count, block, bit
+        self.small = small
+        self.small_arrived = None if small is None else exchange(small, count, bit)
 
     def done(self):
         return self.bit * 2 >= self.count
@@ -630,13 +635,19 @@
             return after
         self.bit *= 2
         which = ((self.index // self.bit) % 2).astype(jnp.int32).reshape(1)
-        sent, self.kept = step_call(which, self.kept, self.arrived, self.block, after)
-        self.arrived = [exchange(sent, self.count, self.bit)]
+        small = () if self.small is None else (self.small, self.small_arrived)
+        sent, kept, *small = step_call(which, self.parts, self.block, after, small)
+        self.parts = [(kept, exchange(sent, self.count, self.bit))]
+        if small:
+            self.small = small[0]
+            self.small_arrived = exchange(self.small, self.count, self.bit)
         return (sent,)
 
-    def total(self):
-        arrived = self.arrived[0] if len(self.arrived) == 1 else jnp.concatenate(self.arrived, axis=1)
-        return self.kept.astype(f32) + arrived.astype(f32)
+    def total(self, after):
+        kept, arrived = self.parts[0]
+        if self.bit > 1:
+            arrived = lax.optimization_barrier((arrived, after[0]))[0]
+        return kept.astype(f32) + arrived.astype(f32)
 
 
 def segments(lengths, row_count):
@@ -730,16 +741,15 @@
 
     bit = (index % 2).astype(jnp.int32).reshape(1)
     block = model // dp_count
-    cut = max(LANES, ff2 * 3 // 8 // LANES * LANES)
-
-    def reduction(pairs, most, after=()):
+
+    def reduction(pairs, most, after=(), small=None):
         sent, kept = weight_halves(pairs, bit, block, most, after)
-        return Reduction(sent, kept, index, dp_count, block)
-
-    ffn_a = reduction([(dout_rows, hidden, 0, cut)], 768)
-    ffn_b = reduction([(dout_rows, hidden, cut, ff2 // 2), (n2, dgu, 0, ff2)], 768, (ffn_a.kept,))
-    order = ffn_a.step((ffn_b.kept,))
-    order = ffn_b.step(order)
+        parts = [(stay, exchange(go, dp_count, 1)) for go, stay in zip(sent, kept)]
+        return Reduction(parts, index, dp_count, block, 1, small)
+
+    ffn_a = reduction([(dout_rows, hidden, 0, ff2 // 2)], 512)
+    ffn_b = reduction([(n2, dgu, 0, ff2)], 2048, (ffn_a.parts[0][0],))
+    order = ffn_a.step((ffn_b.parts[0][0],))
 
     dh1_share, ffn_send, dmix, dy, da, gn2 = call(
         functools.partial(attend_back_kernel, dims, share),
@@ -754,79 +764,65 @@
         1, order, 40 * COST_US,
     )
     order = ffn_a.step((dmix,))
+    order = ffn_b.step(order)
     mix_out = reduction([(dmix, cat, 0, wp + qwp)], 2048, order)
-    mix_a = reduction([(act, da, 0, wp + qwp + LANES)], 2048, (mix_out.kept,))
-    order = ffn_b.step((mix_a.kept,))
+    mix_a = reduction([(act, da, 0, wp + qwp + LANES)], 2048, (mix_out.parts[0][0],))
+    order = ffn_a.step((mix_a.parts[0][0],))
     order = mix_out.step(order)
-
-    dxb, dact, gn1, gcx, gcs, gstep, gskip = call(
-        functools.partial(mixer_back_kernel, dims),
-        [
-            ((rows, wp + 384), bf16), ((rows, model), bf16),
-            ((1, model), f32), ((4, wp), f32), ((4, 256), f32), ((2, LANES), f32), ((1, wp), f32),
-        ],
+    ffn_arrived = swap(ffn_send) if tensor_count == 2 else ffn_send
+
+    dxb, dact, dact_send, small = call(
+        functools.partial(mixer_back_kernel, dims, share),
+        [((rows, wp + 384), bf16), ((rows, model), bf16), ((share, model), bf16), ((8, model), f32)],
         [
             ((rows, rows), f32), ((rows, rows), f32), ((rows, rows), f32), ((rows, wp), f32), ((rows, wp), f32),
         ],
         (
-            pb, dy, y, wzx, state_in, wsp, da, wq, x_rows, seq_col, seq_row, masks, taps, conv_state, bias, rate, skip,
+            place, pb, dy, y, wzx, state_in, wsp, da, wq, x_rows, seq_col, seq_row, masks, taps, conv_state, bias, rate,
+            skip, gn2,
         ),
-        0, order, 40 * COST_US,
+        1, order + (ffn_arrived,), 40 * COST_US,
     )
-    shared = jnp.concatenate([gn1[0], gn2[0] * (1.0 / tensor_count), gcs.reshape(-1)]).reshape(-1, LANES)
-    local = jnp.concatenate([gcx.reshape(-1), gskip.reshape(-1), gstep.reshape(-1)]).reshape(-1, LANES)
-    shared_rows = shared.shape[0]
-    minor = jnp.concatenate([shared, local], axis=0)
-
-    def minor_step(values, bit, after):
-        arrived = exchange(values, dp_count, bit)
-        return call(add_kernel, [(values.shape, f32)], [], (values, arrived), 0, after)[0]
-
-    order = mix_out.step((dxb,))
+    order = ffn_b.step((dxb,))
+    order = mix_out.step(order)
     order = mix_a.step(order)
-    mix_b = reduction([(act, dxb, 0, wp + 384)], 2048, order)
-    order = mix_b.step((mix_b.kept,))
-    minor_bit = 1
-    for r in [ffn_a, ffn_b, mix_a, mix_out, mix_b, mix_a] + 4 * [ffn_a, ffn_b, mix_out, mix_a, mix_b]:
-        if r.done():
-            continue
-        if minor_bit < dp_count:
-            minor = minor_step(minor, minor_bit, order)
-            minor_bit *= 2
-            order = (minor,)
+    mix_b = reduction([(act, dxb, 0, wp + 384)], 384, order, small)
+    order = mix_b.step((mix_b.parts[0][0],))
+    order = ffn_b.step(order)
+    order = mix_a.step(order)
+    order = mix_out.step(order)
+    if tensor_count == 2:
+        dact_mine = lax.dynamic_slice_in_dim(dact, me * share, share, 0).astype(f32)
+        dact_share = dact_mine + lax.optimization_barrier((swap(dact_send), order[0]))[0].astype(f32)
+    else:
+        dact_share = scatter_rows(dact, me, tensor_count)
+    for r in [mix_b, mix_a] + 4 * [ffn_a, ffn_b, mix_out, mix_a, mix_b]:
         order = r.step(order)
-    while minor_bit < dp_count:
-        minor = minor_step(minor, minor_bit, order)
-        minor_bit *= 2
-    ffn_a, ffn_b, mix_a, mix_b = ffn_a.total(), ffn_b.total(), mix_a.total(), mix_b.total()
-    out_total, first_total = mix_out.total(), mix_a
-    down_total = jnp.concatenate([ffn_a, ffn_b[:, : ff2 // 2 - cut]], axis=1)
-    up_total = ffn_b[:, ff2 // 2 - cut :]
+    down_total, up_total = ffn_a.total(order), ffn_b.total(order)
+    out_total, first_total = mix_out.total(order), mix_a.total(order)
+    mix_b, minor = mix_b.total(order), mix_b.small + mix_b.small_arrived
     second_total, state_total = mix_b[:, :wp], mix_b[:, wp : wp + 256]
     step_total = mix_b[:, wp + 256 :]
 
     if tensor_count == 2:
         ffn_mine = lax.dynamic_slice_in_dim(ffn_part, me * share, share, 0).astype(f32)
-        ffn_share = ffn_mine + lax.optimization_barrier((swap(ffn_send), dxb))[0].astype(f32)
+        ffn_share = ffn_mine + ffn_arrived.astype(f32)
     else:
         ffn_share = scatter_rows(ffn_part, me, tensor_count)
     h1_share = lax.dynamic_slice_in_dim(h1, me * share, share, 0)
     block_out = ((h1_share + ffn_share) * live_share).astype(bf16)
 
-    dact_share = scatter_rows(dact, me, tensor_count)
     x_share = tokens.astype(f32)
     r1 = lax.rsqrt(jnp.mean(x_share * x_share, axis=-1, keepdims=True) + norm_eps)
     u = dact_share * gain1
     token_grad = dh1_share + r1 * u - x_share * (r1 * r1 * r1 * jnp.mean(u * x_share, axis=-1, keepdims=True))
 
-    shared = lax.psum(minor[:shared_rows], "tensor") if tensor_count != 2 else minor[:shared_rows] + swap(minor[:shared_rows])
-    shared = shared.reshape(-1)
-    local = minor[shared_rows:].reshape(-1)
-    g_norm1, g_norm2, g_conv_state = shared[:model], shared[model : 2 * model], shared[2 * model :].reshape(4, 256)
-    g_conv_inner = local[: 4 * wp].reshape(4, wp)[:, :inner]
-    g_skip = jnp.sum(local[4 * wp : 5 * wp].reshape(-1, HD), axis=1)[:heads]
-    g_bias = local[5 * wp : 5 * wp + heads]
-    g_decay = local[5 * wp + LANES : 5 * wp + LANES + heads]
+    shared = minor + swap(minor) if tensor_count == 2 else lax.psum(minor, "tensor")
+    g_norm1, g_norm2, g_conv_state = shared[0], shared[1], shared[2:6, wp : wp + 256]
+    g_conv_inner = minor[2:6, :inner]
+    g_skip = jnp.sum(minor[6, :wp].reshape(-1, HD), axis=1)[:heads]
+    g_bias = minor[6, wp : wp + heads]
+    g_decay = minor[6, wp + LANES : wp + LANES + heads]
 
     both = jnp.concatenate([state_total, first_total[:, wp + qwp :]], axis=1).astype(bf16)
     placed = lambda pair: lax.dynamic_update_slice_in_dim(

time: 244 us -> 232 us (0.951)
  waiting for transfers between devices: 61.1 us -> 54.5 us
  starting transfers between devices: 38.1 us -> 31.9 us
  other arithmetic: 16.1 us -> 13 us
    ppermute x8, waiting for transfers between devices: 30.7 us -> 16.2 us  [swap(): return lax.ppermute(values, 'tensor', [(0, 1), (1, 0)])]
    ppermute x26 -> x27, waiting for transfers between devices: 30.4 us -> 38.4 us  [exchange(): return lax.ppermute(sent, 'dp', partners(count, bit))]
    ppermute x26 -> x27, starting transfers between devices: 26 us -> 21.8 us  [exchange(): return lax.ppermute(sent, 'dp', partners(count, bit))]
    unnamed x114 -> x104, local copies, waits for them, and re-layouts: 19.6 us -> 22.4 us
    pallas_call x8 -> x4, Pallas kernels: 52.4 us -> 52.7 us  [call(): pl.pallas_call(wrapped, out_shape=[jax.ShapeDtypeStruct(s, t) for s, t in...]
  transfers between devices with their start and end apart: 34 -> 35, of which waited for: 12 -> 14; matrix products, arithmetic and copies ran while one was open for 15% -> 14% of each run, Pallas kernels for 31% -> 32%
where the time goes in v2:
time: 232 us; the launch traced here: 229 us
  Pallas kernels  94.8 us (41%)
  waiting for transfers between devices  54.5 us (23%)
  starting transfers between devices  31.9 us (14%)
  local copies, waits for them, and re-layouts  30.6 us (13%)
  other arithmetic  13 us (6%)
    pallas_call x4, Pallas kernels, call(): pl.pallas_call(wrapped, out_shape=[jax.ShapeDtypeStruct(s, t) for s, t in...  52.7 us
    ppermute x27, waiting for transfers between devices, exchange(): return lax.ppermute(sent, 'dp', partners(count, bit))  38.4 us
    unnamed x104, local copies, waits for them, and re-layouts  22.4 us
    ppermute x27, starting transfers between devices, exchange(): return lax.ppermute(sent, 'dp', partners(count, bit))  21.8 us
    pallas_call x15, Pallas kernels, step_call(): pl.pallas_call(wrapped, out_shape=[jax.ShapeDtypeStruct(half, bf16)] * 2...  21.3 us
    pallas_call x5, Pallas kernels, weight_halves(): pl.pallas_call(wrapped, out_shape=[jax.ShapeDtypeStruct(s, bf16) for s in...  20.8 us
    ppermute x8, waiting for transfers between devices, swap(): return lax.ppermute(values, 'tensor', [(0, 1), (1, 0)])  16.2 us
    ppermute x8, starting transfers between devices, swap(): return lax.ppermute(values, 'tensor', [(0, 1), (1, 0)])  10.1 us
  transfers between devices with their start and end apart: 35, of which 14 were waited for; matrix products, arithmetic and copies ran while one was open for 14% of the time, Pallas kernels for 32%

profile of v2, /device:TPU:0, one launch (start us, length us, event | category | flops | bytes accessed | tf_op | source)
XLA Modules:
  0.0 228.8 jit_solution(12604910647641874896)
XLA Ops:
  0.7 3.0 %collective-permute-start = (bf16[192,1024]{1,0:T(8,128)(2,1)}, bf16[192,1024]{1,0:T(8,128)(2,1)S(1)}, u32[]{:S(2)}, u32[]{:S(2)}) collective-permute-start(bf16[192,1024]{1,0:T(8,128)(2,1)} %refs_1_.1), channel_id=1, source_target_pairs={{0,1},{1,0},{2,3},{3,2},{4,5},{5,4},{6,7},{7,6},{8,9},{9,8},{10,11... | collective-permute-start | bytes 1179656 | tf_op jit(solution)/shard_map/ppermute | solution.py:591
  8.4 4.2 %copy.57 = bf16[128,8,2,768]{3,1,2,0:T(8,128)(2,1)} copy(bf16[128,8,2,768]{3,2,1,0:T(2,128)(2,1)} %bitcast.36) | data formatting | bytes 6291456
  14.8 16.6 %shard_map.322 = (bf16[384,1024]{1,0:T(8,128)(2,1)}, bf16[384,1024]{1,0:T(8,128)(2,1)}, f32[384,1152]{1,0:T(8,128)}, f32[384,1152]{1,0:T(8,128)}, f32[384,768]{1...) custom-call(s32[2]{0:T(128)S(1)} %pad_add_fusion.refs_0_, bf16[192,1024]{1,0:T(8,128)(2,1)S(1)} %copy-done.6, ...), custom_call_target="tpu_custom_call" | custom-call | flops 11000000512 | bytes 1000 | tf_op jit(solution)/shard_map/pallas_call | solution.py:580
  31.5 1.9 collective-permute-start.1
  33.4 3.4 %copy.58 = bf16[128,8,2,1024]{3,1,2,0:T(8,128)(2,1)} copy(bf16[128,8,2,1024]{3,2,1,0:T(2,128)(2,1)S(1)} %bitcast.35) | data formatting | bytes 8388608
  38.4 2.1 fusion.15.refs_6_
  40.5 10.1 %collective-permute-done.1.refs_2_ = bf16[384,1024]{1,0:T(8,128)(2,1)S(1)} collective-permute-done((bf16[384,1024]{1,0:T(8,128)(2,1)}, bf16[384,1024]{1,0:T(8,128)(2,1)S(1)}, u32[]{:S(2)}, u32[]{:S(2)}) %collective-permute-start.1) | collective-permute-done | bytes 786464 | tf_op jit(solution)/shard_map/ppermute | solution.py:591
  51.5 8.9 %shard_map.323 = (f32[384,1024]{1,0:T(8,128)}, bf16[384,1024]{1,0:T(8,128)(2,1)S(1)}, bf16[384,1024]{1,0:T(8,128)(2,1)S(1)}, bf16[384,2048]{1,0:T(8,128)(2,1)}, ...) custom-call(bf16[384,1024]{1,0:T(8,128)(2,1)} %get-tuple-element.98.refs_0_.refs_9_, ...), custom_call_target="tpu_custom_call" | custom-call | flops 1000 | bytes 1000 | tf_op jit(solution)/shard_map/pallas_call | solution.py:580
  62.9 4.0 %shard_map.324 = (bf16[512,512]{1,0:T(8,128)(2,1)S(1)}, bf16[512,512]{1,0:T(8,128)(2,1)S(1)}, bf16[512,512]{1,0:T(8,128)(2,1)S(1)}, bf16[512,512]{1,0:T(8,128)(2,1)}) custom-call(s32[1]{0:T(128)} %bitcast.11.bit_ref, bf16[384,1024]{1,0:T(8,128)(2,1)} %copy-done.36, bf16[384,1024]{1,0:T(8,128)(2,1)} %copy-done.10), custom_call_target="tpu_custom_call" | custom-call | flops 1000 | bytes 1000 | tf_op jit(solution)/shard_map/pallas_call | solution.py:431
  67.5 5.8 %shard_map.325 = (bf16[512,2048]{1,0:T(8,128)(2,1)}, bf16[512,2048]{1,0:T(8,128)(2,1)}) custom-call(s32[1]{0:T(128)} %bitcast.11.bit_ref, bf16[384,1024]{1,0:T(8,128)(2,1)S(1)} %get-tuple-element.112.refs_0_, bf16[384,2048]{1,0:T(8,128)(2,1)} %get-tuple-element.113.refs_1_, bf16[512,512]{1,0:T(8,128)(2,1)S(1)} %get-tuple-element.108.refs_2_.refs_0_), custom_call_target="tpu_custom_call" | custom-call | flops 1000 | bytes 1000 | tf_op jit(solution)/shard_map/pallas_call | solution.py:431
  76.8 2.7 %collective-permute-done.3.refs_2_ = bf16[384,1024]{1,0:T(8,128)(2,1)} collective-permute-done((bf16[384,1024]{1,0:T(8,128)(2,1)}, bf16[384,1024]{1,0:T(8,128)(2,1)}, u32[]{:S(2)}, u32[]{:S(2)}) %collective-permute-start.3) | collective-permute-done | bytes 786464 | tf_op jit(solution)/shard_map/ppermute | solution.py:591
  79.5 12.5 %shard_map.327 = (f32[192,1024]{1,0:T(8,128)}, bf16[192,1024]{1,0:T(8,128)(2,1)}, bf16[384,1024]{1,0:T(8,128)(2,1)}, f32[384,768]{1,0:T(8,128)}, bf16[384,1152]{1,0:T(8,128)(2,1)}, /*index=5*/f32[1,1024]{1,0:T(1,128)S(1)}) custom-call(s32[2]{0:T(128)S(1)} %pad_add_fusion.refs_0_, bf16[384,1024]{1,0:T(8,128)(2,1)} %get-tuple-element.104.refs_1_, ...), custom_call_target="tpu_custom_call" | custom-call | flops 44000002048 | bytes 1000 | tf_op jit(solution)/shard_map/pallas_call | solution.py:580
  94.4 3.4 %shard_map.329 = (bf16[256,2048]{1,0:T(8,128)(2,1)S(1)}, bf16[256,2048]{1,0:T(8,128)(2,1)}) custom-call(s32[1]{0:T(128)} %bitcast.10.which_ref, bf16[512,2048]{1,0:T(8,128)(2,1)} %get-tuple-element.114.refs_4_.refs_0_, bf16[512,2048]{1,0:T(8,128)(2,1)} %copy-done.37, bf16[128,1024]{1,0:T(8,128)(2,1)} %get-tuple-element.126.refs_2_), custom_call_target="tpu_custom_call" | custom-call | flops 1000 | bytes 1000 | tf_op jit(solution)/shard_map/pallas_call | solution.py:496
  98.7 3.1 %shard_map.330 = (bf16[512,1024]{1,0:T(8,128)(2,1)}, bf16[512,1024]{1,0:T(8,128)(2,1)}) custom-call(s32[1]{0:T(128)} %bitcast.11.bit_ref, bf16[384,1024]{1,0:T(8,128)(2,1)S(1)} %copy-done.5, bf16[384,1024]{1,0:T(8,128)(2,1)S(1)} %copy-done.11, bf16[256,2048]{1,0:T(8,128)(2,1)} %copy-done.7), custom_call_target="tpu_custom_call" | custom-call | flops 1000 | bytes 1000 | tf_op jit(solution)/shard_map/pallas_call | solution.py:431
  106.6 3.5 %shard_map.331 = (bf16[512,1152]{1,0:T(8,128)(2,1)}, bf16[512,1152]{1,0:T(8,128)(2,1)}) custom-call(s32[1]{0:T(128)} %bitcast.11.bit_ref, bf16[384,1024]{1,0:T(8,128)(2,1)S(1)} %copy-done.4, bf16[384,1152]{1,0:T(8,128)(2,1)S(1)} %copy-done.9, bf16[512,1024]{1,0:T(8,128)(2,1)} %get-tuple-element.128.refs_2_.refs_0_), custom_call_target="tpu_custom_call" | custom-call | flops 1000 | bytes 1000 | tf_op jit(solution)/shard_map/pallas_call | solution.py:431
  110.1 2.1 collective-permute-done.10.refs_1_
  114.7 1.8 shard_map.333
  118.2 14.6 %shard_map.334 = (bf16[384,1152]{1,0:T(8,128)(2,1)}, bf16[384,1024]{1,0:T(8,128)(2,1)}, bf16[192,1024]{1,0:T(8,128)(2,1)}, f32[8,1024]{1,0:T(8,128)S(1)}) custom-call(s32[2]{0:T(128)S(1)} %pad_add_fusion.refs_0_, f32[384,1152]{1,0:T(8,128)} %get-tuple-element.118.refs_1_, f32[384,768]{1,0:T(8,128)} %get-tuple-element.119.refs_2_, ...), custom_call_target="tpu_custom_call" | custom-call | flops 44000002048 | bytes 1000 | tf_op jit(solution)/shard_map/pallas_call | solution.py:580
  137.6 3.7 %collective-permute-done.12.refs_1_ = bf16[256,1024]{1,0:T(8,128)(2,1)S(1)} collective-permute-done((bf16[256,1024]{1,0:T(8,128)(2,1)S(1)}, bf16[256,1024]{1,0:T(8,128)(2,1)S(1)}, u32[]{:S(2)}, u32[]{:S(2)}) %collective-permute-start.12) | collective-permute-done | bytes 524320 | tf_op jit(solution)/shard_map/ppermute | solution.py:621
  143.3 2.0 shard_map.337
  146.2 4.5 %shard_map.338 = (bf16[512,384]{1,0:T(8,128)(2,1)S(1)}, bf16[512,384]{1,0:T(8,128)(2,1)S(1)}, bf16[512,384]{1,0:T(8,128)(2,1)S(1)}, bf16[512,384]{1,0:T(8,128)(2...) custom-call(s32[1]{0:T(128)} %bitcast.11.bit_ref, bf16[384,1024]{1,0:T(8,128)(2,1)} %get-tuple-element.131.refs_0_, ...), custom_call_target="tpu_custom_call" | custom-call | flops 1000 | bytes 1000 | tf_op jit(solution)/shard_map/pallas_call | solution.py:431
  155.2 2.5 %shard_map.339 = (bf16[256,1152]{1,0:T(8,128)(2,1)}, bf16[256,1152]{1,0:T(8,128)(2,1)}, f32[8,1024]{1,0:T(8,128)S(1)}) custom-call(s32[1]{0:T(128)} %bitcast.10.which_ref, bf16[512,384]{1,0:T(8,128)(2,1)S(1)} %get-tuple-element.147.refs_0_.refs_8_, bf16[512,384]{1,0:T(8,128)(2,1)S(1)} %collective-permute-done.18.refs_1_, ...), custom_call_target="tpu_custom_call" | custom-call | flops 1000 | bytes 1000 | tf_op jit(solution)/shard_map/pallas_call | solution.py:496
  161.7 2.2 multiply_convert_fusion
  164.0 4.9 %collective-permute-done.17.refs_1_ = bf16[128,2048]{1,0:T(8,128)(2,1)} collective-permute-done((bf16[128,2048]{1,0:T(8,128)(2,1)S(1)}, bf16[128,2048]{1,0:T(8,128)(2,1)}, u32[]{:S(2)}, u32[]{:S(2)}) %collective-permute-start.17) | collective-permute-done | bytes 524320 | tf_op jit(solution)/shard_map/ppermute | solution.py:621
  168.9 2.6 %collective-permute-start.34 = (bf16[64,1024]{1,0:T(8,128)(2,1)S(1)}, bf16[64,1024]{1,0:T(8,128)(2,1)S(1)}, u32[]{:S(2)}, u32[]{:S(2)}) collective-permute-start(bf16[64,1024]{1,0:T(8,128)(2,1)S(1)} %copy-done.24), channel_id=1, source_target_pairs={{0,16},{2,18},{4,20},{6,22},{8,24},{10,26},{12,28},{14,30},{16,0},... | collective-permute-start | bytes 393224 | tf_op jit(solution)/shard_map/ppermute | solution.py:621
  174.7 2.8 %collective-permute-done.14.refs_1_ = bf16[128,1024]{1,0:T(8,128)(2,1)} collective-permute-done((bf16[128,1024]{1,0:T(8,128)(2,1)}, bf16[128,1024]{1,0:T(8,128)(2,1)}, u32[]{:S(2)}, u32[]{:S(2)}) %collective-permute-start.14) | collective-permute-done | bytes 262176 | tf_op jit(solution)/shard_map/ppermute | solution.py:621
  181.9 1.8 collective-permute-start.24
  184.0 11.9 %collective-permute-done.26.refs_1_ = bf16[128,1152]{1,0:T(8,128)(2,1)S(1)} collective-permute-done((bf16[128,1152]{1,0:T(8,128)(2,1)S(1)}, bf16[128,1152]{1,0:T(8,128)(2,1)S(1)}, u32[]{:S(2)}, u32[]{:S(2)}) %collective-permute-start.26) | collective-permute-done | bytes 294944 | tf_op jit(solution)/shard_map/ppermute | solution.py:621
  196.4 2.1 fusion.4
  198.4 2.4 %collective-permute-done.25.refs_3_ = f32[8,1024]{1,0:T(8,128)S(1)} collective-permute-done((f32[8,1024]{1,0:T(8,128)S(1)}, f32[8,1024]{1,0:T(8,128)S(1)}, u32[]{:S(2)}, u32[]{:S(2)}) %collective-permute-start.25) | collective-permute-done | bytes 32800 | tf_op jit(solution)/shard_map/ppermute | solution.py:621
  200.9 2.3 %collective-permute-start.32 = (bf16[64,1024]{1,0:T(8,128)(2,1)S(1)}, bf16[64,1024]{1,0:T(8,128)(2,1)S(1)}, u32[]{:S(2)}, u32[]{:S(2)}) collective-permute-start(bf16[64,1024]{1,0:T(8,128)(2,1)S(1)} %get-tuple-element.157.refs_4_), channel_id=1, source_target_pairs={{0,16},{2,18},{4,20},{6,22},{8,24},{10,26},{12,28},{14,30},{16,0},... | collective-permute-start | bytes 393224 | tf_op jit(solution)/shard_map/ppermute | solution.py:621
  204.3 8.5 %collective-permute-done.32 = bf16[64,1024]{1,0:T(8,128)(2,1)S(1)} collective-permute-done((bf16[64,1024]{1,0:T(8,128)(2,1)S(1)}, bf16[64,1024]{1,0:T(8,128)(2,1)S(1)}, u32[]{:S(2)}, u32[]{:S(2)}) %collective-permute-start.32) | collective-permute-done | bytes 131104 | tf_op jit(solution)/shard_map/ppermute | solution.py:621
  (226 shorter events, 68.9 us)
Async XLA Ops:
  0.7 13.8 %collective-permute-start = (bf16[192,1024]{1,0:T(8,128)(2,1)}, bf16[192,1024]{1,0:T(8,128)(2,1)S(1)}, u32[]{:S(2)}, u32[]{:S(2)}) collective-permute-start(bf16[192,1024]{1,0:T(8,128)(2,1)} %refs_1_.1), channel_id=1, source_target_pairs={{0,1},{1,0},{2,3},{3,2},{4,5},{5,4},{6,7},{7,6},{8,9},{9,8},{10,11... | collective-permute-start | bytes 1179656 | tf_op jit(solution)/shard_map/ppermute | solution.py:591
  14.5 22.3 %collective-permute-start.2 = (bf16[192,1024]{1,0:T(8,128)(2,1)S(1)}, bf16[192,1024]{1,0:T(8,128)(2,1)S(1)}, u32[]{:S(2)}, u32[]{:S(2)}) collective-permute-start(bf16[192,1024]{1,0:T(8,128)(2,1)S(1)} %copy-done.45), channel_id=1, source_target_pairs={{0,1},{1,0},{2,3},{3,2},{4,5},{5,4},{6,7},{7,6},{8,9},{9,8},{10,11... | collective-permute-start | bytes 1179656 | tf_op jit(solution)/shard_map/ppermute | solution.py:591
  31.5 19.1 %collective-permute-start.1 = (bf16[384,1024]{1,0:T(8,128)(2,1)}, bf16[384,1024]{1,0:T(8,128)(2,1)S(1)}, u32[]{:S(2)}, u32[]{:S(2)}) collective-permute-start(bf16[384,1024]{1,0:T(8,128)(2,1)} %get-tuple-element.99.refs_1_), channel_id=1, source_target_pairs={{0,1},{1,0},{2,3},{3,2},{4,5},{5,4},{6,7},{7,6},{8,9},{9,8},{10,11... | collective-permute-start | bytes 2359304 | tf_op jit(solution)/shard_map/ppermute | solution.py:591
  61.2 18.2 %collective-permute-start.3 = (bf16[384,1024]{1,0:T(8,128)(2,1)}, bf16[384,1024]{1,0:T(8,128)(2,1)}, u32[]{:S(2)}, u32[]{:S(2)}) collective-permute-start(bf16[384,1024]{1,0:T(8,128)(2,1)} %get-tuple-element.104.refs_1_), channel_id=1, source_target_pairs={{0,1},{1,0},{2,3},{3,2},{4,5},{5,4},{6,7},{7,6},{8,9},{9,8},{10,11... | collective-permute-start | bytes 2359304 | tf_op jit(solution)/shard_map/ppermute | solution.py:591
  66.9 6.5 %collective-permute-start.4 = (bf16[512,512]{1,0:T(8,128)(2,1)S(1)}, bf16[512,512]{1,0:T(8,128)(2,1)}, u32[]{:S(2)}, u32[]{:S(2)}) collective-permute-start(bf16[512,512]{1,0:T(8,128)(2,1)S(1)} %get-tuple-element.109), channel_id=1, source_target_pairs={{0,2},{2,0},{4,6},{6,4},{8,10},{10,8},{12,14},{14,12},{16,18},{18,... | collective-permute-start | bytes 1572872 | tf_op jit(solution)/shard_map/ppermute | solution.py:621
  67.0 6.5 %collective-permute-start.5 = (bf16[512,512]{1,0:T(8,128)(2,1)S(1)}, bf16[512,512]{1,0:T(8,128)(2,1)}, u32[]{:S(2)}, u32[]{:S(2)}) collective-permute-start(bf16[512,512]{1,0:T(8,128)(2,1)S(1)} %get-tuple-element.111), channel_id=1, source_target_pairs={{0,2},{2,0},{4,6},{6,4},{8,10},{10,8},{12,14},{14,12},{16,18},{18,... | collective-permute-start | bytes 1572872 | tf_op jit(solution)/shard_map/ppermute | solution.py:621
  73.3 19.7 %collective-permute-start.7 = (bf16[512,2048]{1,0:T(8,128)(2,1)}, bf16[512,2048]{1,0:T(8,128)(2,1)S(1)}, u32[]{:S(2)}, u32[]{:S(2)}) collective-permute-start(bf16[512,2048]{1,0:T(8,128)(2,1)} %get-tuple-element.124), channel_id=1, source_target_pairs={{0,2},{2,0},{4,6},{6,4},{8,10},{10,8},{12,14},{14,12},{16,18},{18,... | collective-permute-start | bytes 6291464 | tf_op jit(solution)/shard_map/ppermute | solution.py:621
  75.2 16.9 %collective-permute-start.8 = (bf16[256,1024]{1,0:T(8,128)(2,1)S(1)}, bf16[256,1024]{1,0:T(8,128)(2,1)S(1)}, u32[]{:S(2)}, u32[]{:S(2)}) collective-permute-start(bf16[256,1024]{1,0:T(8,128)(2,1)S(1)} %get-tuple-element.115.refs_15_), channel_id=1, source_target_pairs={{0,4},{2,6},{4,0},{6,2},{8,12},{10,14},{12,8},{14,10},{16,20},{18,... | collective-permute-start | bytes 1572872 | tf_op jit(solution)/shard_map/ppermute | solution.py:621
  101.8 12.9 %collective-permute-start.9 = (bf16[512,1024]{1,0:T(8,128)(2,1)}, bf16[512,1024]{1,0:T(8,128)(2,1)}, u32[]{:S(2)}, u32[]{:S(2)}) collective-permute-start(bf16[512,1024]{1,0:T(8,128)(2,1)} %get-tuple-element.129), channel_id=1, source_target_pairs={{0,2},{2,0},{4,6},{6,4},{8,10},{10,8},{12,14},{14,12},{16,18},{18,... | collective-permute-start | bytes 3145736 | tf_op jit(solution)/shard_map/ppermute | solution.py:621
  101.9 16.3 %collective-permute-start.6 = (bf16[192,1024]{1,0:T(8,128)(2,1)}, bf16[192,1024]{1,0:T(8,128)(2,1)}, u32[]{:S(2)}, u32[]{:S(2)}) collective-permute-start(bf16[192,1024]{1,0:T(8,128)(2,1)} %get-tuple-element.116), channel_id=1, source_target_pairs={{0,1},{1,0},{2,3},{3,2},{4,5},{5,4},{6,7},{7,6},{8,9},{9,8},{10,11... | collective-permute-start | bytes 1179656 | tf_op jit(solution)/shard_map/ppermute | solution.py:591
  103.5 8.7 %collective-permute-start.10 = (bf16[128,1024]{1,0:T(8,128)(2,1)}, bf16[128,1024]{1,0:T(8,128)(2,1)}, u32[]{:S(2)}, u32[]{:S(2)}) collective-permute-start(bf16[128,1024]{1,0:T(8,128)(2,1)} %get-tuple-element.126.refs_2_), channel_id=1, source_target_pairs={{0,8},{2,10},{4,12},{6,14},{8,0},{10,2},{12,4},{14,6},{16,24},{18,... | collective-permute-start | bytes 786440 | tf_op jit(solution)/shard_map/ppermute | solution.py:621
  105.1 27.7 %collective-permute-start.13 = (bf16[256,2048]{1,0:T(8,128)(2,1)S(1)}, bf16[256,2048]{1,0:T(8,128)(2,1)S(1)}, u32[]{:S(2)}, u32[]{:S(2)}) collective-permute-start(bf16[256,2048]{1,0:T(8,128)(2,1)S(1)} %copy-done.8), channel_id=1, source_target_pairs={{0,4},{2,6},{4,0},{6,2},{8,12},{10,14},{12,8},{14,10},{16,20},{18,... | collective-permute-start | bytes 3145736 | tf_op jit(solution)/shard_map/ppermute | solution.py:621
  110.1 32.2 %collective-permute-start.15 = (bf16[512,1152]{1,0:T(8,128)(2,1)}, bf16[512,1152]{1,0:T(8,128)(2,1)S(1)}, u32[]{:S(2)}, u32[]{:S(2)}) collective-permute-start(bf16[512,1152]{1,0:T(8,128)(2,1)} %get-tuple-element.143), channel_id=1, source_target_pairs={{0,2},{2,0},{4,6},{6,4},{8,10},{10,8},{12,14},{14,12},{16,18},{18,... | collective-permute-start | bytes 3538952 | tf_op jit(solution)/shard_map/ppermute | solution.py:621
  116.6 24.7 %collective-permute-start.12 = (bf16[256,1024]{1,0:T(8,128)(2,1)S(1)}, bf16[256,1024]{1,0:T(8,128)(2,1)S(1)}, u32[]{:S(2)}, u32[]{:S(2)}) collective-permute-start(bf16[256,1024]{1,0:T(8,128)(2,1)S(1)} %get-tuple-element.134.refs_19_), channel_id=1, source_target_pairs={{0,4},{2,6},{4,0},{6,2},{8,12},{10,14},{12,8},{14,10},{16,20},{18,... | collective-permute-start | bytes 1572872 | tf_op jit(solution)/shard_map/ppermute | solution.py:621
  150.7 3.8 %collective-permute-start.18 = (bf16[512,384]{1,0:T(8,128)(2,1)S(1)}, bf16[512,384]{1,0:T(8,128)(2,1)S(1)}, u32[]{:S(2)}, u32[]{:S(2)}) collective-permute-start(bf16[512,384]{1,0:T(8,128)(2,1)S(1)} %get-tuple-element.148), channel_id=1, source_target_pairs={{0,2},{2,0},{4,6},{6,4},{8,10},{10,8},{12,14},{14,12},{16,18},{18,... | collective-permute-start | bytes 1179656 | tf_op jit(solution)/shard_map/ppermute | solution.py:621
  151.3 21.6 %collective-permute-start.16 = (bf16[256,1152]{1,0:T(8,128)(2,1)S(1)}, bf16[256,1152]{1,0:T(8,128)(2,1)}, u32[]{:S(2)}, u32[]{:S(2)}) collective-permute-start(bf16[256,1152]{1,0:T(8,128)(2,1)S(1)} %copy-done.13), channel_id=1, source_target_pairs={{0,4},{2,6},{4,0},{6,2},{8,12},{10,14},{12,8},{14,10},{16,20},{18,... | collective-permute-start | bytes 1769480 | tf_op jit(solution)/shard_map/ppermute | solution.py:621
  154.0 14.9 %collective-permute-start.17 = (bf16[128,2048]{1,0:T(8,128)(2,1)S(1)}, bf16[128,2048]{1,0:T(8,128)(2,1)}, u32[]{:S(2)}, u32[]{:S(2)}) collective-permute-start(bf16[128,2048]{1,0:T(8,128)(2,1)S(1)} %copy-done.16), channel_id=1, source_target_pairs={{0,8},{2,10},{4,12},{6,14},{8,0},{10,2},{12,4},{14,6},{16,24},{18,... | collective-permute-start | bytes 1572872 | tf_op jit(solution)/shard_map/ppermute | solution.py:621
  157.7 23.7 %collective-permute-start.22 = (bf16[256,1152]{1,0:T(8,128)(2,1)}, bf16[256,1152]{1,0:T(8,128)(2,1)S(1)}, u32[]{:S(2)}, u32[]{:S(2)}) collective-permute-start(bf16[256,1152]{1,0:T(8,128)(2,1)} %get-tuple-element.154.refs_2_), channel_id=1, source_target_pairs={{0,4},{2,6},{4,0},{6,2},{8,12},{10,14},{12,8},{14,10},{16,20},{18,... | collective-permute-start | bytes 1769480 | tf_op jit(solution)/shard_map/ppermute | solution.py:621
  158.9 20.8 %collective-permute-start.11 = (bf16[192,1024]{1,0:T(8,128)(2,1)}, bf16[192,1024]{1,0:T(8,128)(2,1)}, u32[]{:S(2)}, u32[]{:S(2)}) collective-permute-start(bf16[192,1024]{1,0:T(8,128)(2,1)} %get-tuple-element.136), channel_id=1, source_target_pairs={{0,1},{1,0},{2,3},{3,2},{4,5},{5,4},{6,7},{7,6},{8,9},{9,8},{10,11... | collective-permute-start | bytes 1179656 | tf_op jit(solution)/shard_map/ppermute | solution.py:591
  159.4 18.1 %collective-permute-start.14 = (bf16[128,1024]{1,0:T(8,128)(2,1)}, bf16[128,1024]{1,0:T(8,128)(2,1)}, u32[]{:S(2)}, u32[]{:S(2)}) collective-permute-start(bf16[128,1024]{1,0:T(8,128)(2,1)} %get-tuple-element.142.refs_2_), channel_id=1, source_target_pairs={{0,8},{2,10},{4,12},{6,14},{8,0},{10,2},{12,4},{14,6},{16,24},{18,... | collective-permute-start | bytes 786440 | tf_op jit(solution)/shard_map/ppermute | solution.py:621
  168.9 35.3 %collective-permute-start.34 = (bf16[64,1024]{1,0:T(8,128)(2,1)S(1)}, bf16[64,1024]{1,0:T(8,128)(2,1)S(1)}, u32[]{:S(2)}, u32[]{:S(2)}) collective-permute-start(bf16[64,1024]{1,0:T(8,128)(2,1)S(1)} %copy-done.24), channel_id=1, source_target_pairs={{0,16},{2,18},{4,20},{6,22},{8,24},{10,26},{12,28},{14,30},{16,0},... | collective-permute-start | bytes 393224 | tf_op jit(solution)/shard_map/ppermute | solution.py:621
  172.9 31.3 %collective-permute-start.33 = (bf16[64,2048]{1,0:T(8,128)(2,1)S(1)}, bf16[64,2048]{1,0:T(8,128)(2,1)S(1)}, u32[]{:S(2)}, u32[]{:S(2)}) collective-permute-start(bf16[64,2048]{1,0:T(8,128)(2,1)S(1)} %get-tuple-element.155.refs_2_), channel_id=1, source_target_pairs={{0,16},{2,18},{4,20},{6,22},{8,24},{10,26},{12,28},{14,30},{16,0},... | collective-permute-start | bytes 786440 | tf_op jit(solution)/shard_map/ppermute | solution.py:621
  177.5 3.9 %collective-permute-start.23 = (f32[8,1024]{1,0:T(8,128)S(1)}, f32[8,1024]{1,0:T(8,128)S(1)}, u32[]{:S(2)}, u32[]{:S(2)}) collective-permute-start(f32[8,1024]{1,0:T(8,128)S(1)} %get-tuple-element.160.refs_2_), channel_id=1, source_target_pairs={{0,4},{2,6},{4,0},{6,2},{8,12},{10,14},{12,8},{14,10},{16,20},{18,... | collective-permute-start | bytes 98312 | tf_op jit(solution)/shard_map/ppermute | solution.py:621
  179.7 16.3 %collective-permute-start.26 = (bf16[128,1152]{1,0:T(8,128)(2,1)S(1)}, bf16[128,1152]{1,0:T(8,128)(2,1)S(1)}, u32[]{:S(2)}, u32[]{:S(2)}) collective-permute-start(bf16[128,1152]{1,0:T(8,128)(2,1)S(1)} %get-tuple-element.156.refs_2_), channel_id=1, source_target_pairs={{0,8},{2,10},{4,12},{6,14},{8,0},{10,2},{12,4},{14,6},{16,24},{18,... | collective-permute-start | bytes 884744 | tf_op jit(solution)/shard_map/ppermute | solution.py:621
  181.9 21.3 %collective-permute-start.24 = (bf16[128,1152]{1,0:T(8,128)(2,1)S(1)}, bf16[128,1152]{1,0:T(8,128)(2,1)S(1)}, u32[]{:S(2)}, u32[]{:S(2)}) collective-permute-start(bf16[128,1152]{1,0:T(8,128)(2,1)S(1)} %get-tuple-element.162.refs_2_), channel_id=1, source_target_pairs={{0,8},{2,10},{4,12},{6,14},{8,0},{10,2},{12,4},{14,6},{16,24},{18,... | collective-permute-start | bytes 884744 | tf_op jit(solution)/shard_map/ppermute | solution.py:621
  183.8 17.1 %collective-permute-start.25 = (f32[8,1024]{1,0:T(8,128)S(1)}, f32[8,1024]{1,0:T(8,128)S(1)}, u32[]{:S(2)}, u32[]{:S(2)}) collective-permute-start(f32[8,1024]{1,0:T(8,128)S(1)} %get-tuple-element.163.refs_2_), channel_id=1, source_target_pairs={{0,8},{2,10},{4,12},{6,14},{8,0},{10,2},{12,4},{14,6},{16,24},{18,... | collective-permute-start | bytes 98312 | tf_op jit(solution)/shard_map/ppermute | solution.py:621
  196.3 7.9 %collective-permute-start.29 = (bf16[64,1152]{1,0:T(8,128)(2,1)S(1)}, bf16[64,1152]{1,0:T(8,128)(2,1)S(1)}, u32[]{:S(2)}, u32[]{:S(2)}) collective-permute-start(bf16[64,1152]{1,0:T(8,128)(2,1)S(1)} %get-tuple-element.165.refs_4_), channel_id=1, source_target_pairs={{0,16},{2,18},{4,20},{6,22},{8,24},{10,26},{12,28},{14,30},{16,0},... | collective-permute-start | bytes 442376 | tf_op jit(solution)/shard_map/ppermute | solution.py:621
  200.9 11.9 %collective-permute-start.32 = (bf16[64,1024]{1,0:T(8,128)(2,1)S(1)}, bf16[64,1024]{1,0:T(8,128)(2,1)S(1)}, u32[]{:S(2)}, u32[]{:S(2)}) collective-permute-start(bf16[64,1024]{1,0:T(8,128)(2,1)S(1)} %get-tuple-element.157.refs_4_), channel_id=1, source_target_pairs={{0,16},{2,18},{4,20},{6,22},{8,24},{10,26},{12,28},{14,30},{16,0},... | collective-permute-start | bytes 393224 | tf_op jit(solution)/shard_map/ppermute | solution.py:621
  203.6 19.2 %collective-permute-start.30 = (bf16[64,1152]{1,0:T(8,128)(2,1)S(1)}, bf16[64,1152]{1,0:T(8,128)(2,1)S(1)}, u32[]{:S(2)}, u32[]{:S(2)}) collective-permute-start(bf16[64,1152]{1,0:T(8,128)(2,1)S(1)} %get-tuple-element.168), channel_id=1, source_target_pairs={{0,16},{2,18},{4,20},{6,22},{8,24},{10,26},{12,28},{14,30},{16,0},... | collective-permute-start | bytes 442376 | tf_op jit(solution)/shard_map/ppermute | solution.py:621
  212.8 4.8 %collective-permute-start.27 = (f32[8,1024]{1,0:T(8,128)S(1)}, f32[8,1024]{1,0:T(8,128)S(1)}, u32[]{:S(2)}, u32[]{:S(2)}) collective-permute-start(f32[8,1024]{1,0:T(8,128)S(1)} %get-tuple-element.166), channel_id=1, source_target_pairs={{0,16},{2,18},{4,20},{6,22},{8,24},{10,26},{12,28},{14,30},{16,0},... | collective-permute-start | bytes 98312 | tf_op jit(solution)/shard_map/ppermute | solution.py:621
  217.6 3.9 %collective-permute-start.28 = (f32[8,1024]{1,0:T(8,128)S(1)}, f32[8,1024]{1,0:T(8,128)S(1)}, u32[]{:S(2)}, u32[]{:S(2)}) collective-permute-start(f32[8,1024]{1,0:T(8,128)S(1)} %add.130), channel_id=1, source_target_pairs={{0,1},{1,0},{2,3},{3,2},{4,5},{5,4},{6,7},{7,6},{8,9},{9,8},{10,11... | collective-permute-start | bytes 98312 | tf_op jit(solution)/shard_map/ppermute | solution.py:591
  222.8 4.2 %collective-permute-start.31 = (bf16[64,384]{1,0:T(8,128)(2,1)S(1)}, bf16[64,384]{1,0:T(8,128)(2,1)S(1)}, u32[]{:S(2)}, u32[]{:S(2)}) collective-permute-start(bf16[64,384]{1,0:T(8,128)(2,1)S(1)} %pad_maximum_fusion.1), channel_id=1, source_target_pairs={{0,1},{1,0},{2,3},{3,2},{4,5},{5,4},{6,7},{7,6},{8,9},{9,8},{10,11... | collective-permute-start | bytes 147464 | tf_op jit(solution)/shard_map/ppermute | solution.py:591
  (52 other events, 349.7 us)
